TPU v7x, 32 devices: a whole 2x2x4 slice. The times are simulated.
32 devices in a mesh: ctx: 8 (over y, x, core), tp: 4 (over z).
Axes of the slice: x: 2, y: 2, z: 4, core: 2. Of those that a mesh axis runs over, the one named last changes fastest.
Arguments:
- tokens: bfloat16 [2048, 8192], P('ctx', 'tp'), may hold values from -6 to 6
- frozen: bfloat16 [2048, 3, 8192], P('ctx', None, 'tp'), may hold values from -3 to 3
- cotangent: bfloat16 [2048, 8192], P('ctx', 'tp'), may hold values from -0.119628906 to 0.119628906
- adapter_down_weight: bfloat16 [16, 8192], P(None, 'tp'), may hold values from -0.0625 to 0.0625
- adapter_up_weight: bfloat16 [16, 3, 8192], P(None, None, 'tp'), may hold values from -0.75 to 0.75
- short_depthwise_filter: bfloat16 [3, 3, 8192], P(None, None, 'tp'), may hold values from -3.5 to 3.5
- long_group_filter: bfloat16 [512, 128], P('tp'), may hold values from -8 to 8
- skip_direct_scale: float32 [8192], P('tp'), may hold values from -3 to 3
- document_lengths: int32 [16], replicated, may hold values from 1 to 1024, 2048 in all
- window_row_position: int32 [2048], P('ctx'), may hold values from 0 to 2047, as said below
Outputs:
- mixer_out: bfloat16 [2048, 8192], P('ctx', 'tp')
- grad_down: float32 [16, 8192], P(None, 'tp')
- up_gradient: float32 [16, 3, 8192], P(None, None, 'tp')
- grad_short: float32 [3, 3, 8192], P(None, None, 'tp')
- grad_long: float32 [512, 128], P('tp')
- grad_skip: float32 [8192], P('tp')
Inputs may be any that keep to these rules, and one draw needn't show every extreme that they name: `window_row_position`: a permutation of the window's positions; the rows of one loader device (one index of ctx) go to each context shard (places j * 256 to (j + 1) * 256 - 1) in a count of 0, 32 or 64, and in a count of 64 to at least one shard. `document_lengths`: the documents lie end to end in the window in this order; the lengths sum to 2048.
All inputs are finite; a program needn't handle non-finite values.
Results may differ from a plain program's by a relative error of at most 0.0055.
The roundings to bfloat16 on the way count: a program that leaves them out, or rounds other values in their place, can miss the bound.
Values may be sent and summed in bfloat16 or wider, within the bound.
A program may use at most 128 MiB of HBM per device.

v0:
```python
import functools

import jax
import jax.numpy as jnp
from jax import lax
from jax.experimental import pallas as pl
from jax.experimental.pallas import tpu as pltpu
from jax.sharding import PartitionSpec as P

EDGE = 16
LANES = 128


def fdot(left, right, contract=((1,), (0,))):
    return lax.dot_general(left, right, (contract, ((), ())), preferred_element_type=jnp.float32)


def doc_starts(pos, lengths_ref):
    begins = jnp.zeros_like(pos)
    running = jnp.int32(0)
    for doc in range(lengths_ref.shape[0]):
        begins = jnp.where(pos >= running, running, begins)
        running = running + lengths_ref[doc]
    return begins


def core_kernel(
    lengths_ref,
    frozen_ref,
    low_ref,
    place_ref,
    cot_ref,
    up_ref,
    short_ref,
    taps_f_ref,
    taps_b_ref,
    skip_ref,
    out_ref,
    up_grad_ref,
    short_grad_ref,
    long_grad_ref,
    skip_grad_ref,
    back_low_ref,
    rhs,
    pre,
    low_win,
    post,
    prod,
    back,
    back_post,
    bank_f,
    bank_b,
    pair_acc,
    start_col,
    start_row,
):
    n, c = cot_ref.shape
    groups, wide = taps_f_ref.shape
    taps = wide // 2
    per = c // groups
    shards, kinds, rows, _ = frozen_ref.shape
    width = kinds * c
    blocks = n // taps
    shorts = short_ref.shape[0]
    f32, bf16 = jnp.float32, jnp.bfloat16

    start_col[...] = doc_starts(
        lax.broadcasted_iota(jnp.int32, start_col.shape, 0), lengths_ref
    )
    start_row[...] = doc_starts(
        lax.broadcasted_iota(jnp.int32, start_row.shape, 1), lengths_ref
    )

    for g in range(groups):
        span = slice(g * taps, (g + 1) * taps)
        for taps_ref, bank in ((taps_f_ref, bank_f), (taps_b_ref, bank_b)):
            line = jnp.broadcast_to(taps_ref[g : g + 1, :], (taps, wide))
            bank[span, :] = pltpu.roll(line, 0, 1, stride=1, stride_axis=0).astype(bf16)

    @pl.loop(0, shards)
    def _(j):
        at = pl.ds(pl.multiple_of(j * rows, rows), rows)
        low = low_ref[at, :]
        for a in range(kinds):
            cols = slice(a * c, (a + 1) * c)
            rhs[at, cols] = (frozen_ref[j, a].astype(f32) + fdot(low, up_ref[:, cols])).astype(bf16)
        rhs[at, width:] = low

    pre[:EDGE, :] = jnp.zeros((EDGE, width), bf16)
    tall = rows * 2

    @pl.loop(0, n // tall)
    def _(w):
        base = pl.multiple_of(w * tall, tall)
        spot = lax.broadcasted_iota(jnp.int32, (tall, n), 0) + base
        hot = jnp.where(place_ref[...] == spot, 1.0, 0.0).astype(bf16)
        moved = fdot(hot, rhs[...]).astype(bf16)
        pre[pl.ds(pl.multiple_of(base + EDGE, EDGE), tall), :] = moved[:, :width]
        low_win[pl.ds(base, tall), :] = moved[:, width:]

    prod[:taps, :] = jnp.zeros((taps, c), bf16)
    back[n:, :] = jnp.zeros((taps, c), bf16)

    @pl.loop(0, blocks)
    def _(b):
        base = pl.multiple_of(b * taps, taps)
        at = pl.ds(base, taps)
        ext = pre[pl.ds(base, taps + EDGE), :].astype(f32)
        off = lax.broadcasted_iota(jnp.int32, (taps, 1), 0) + base - start_col[at, :]
        total = jnp.zeros((taps, width), f32)
        for s in range(shorts):
            gate = (off >= s).astype(f32)
            total = total + short_ref[s : s + 1, :] * ext[EDGE - s : EDGE - s + taps] * gate
        rounded = total.astype(bf16)
        post[at, :] = rounded
        rounded = rounded.astype(f32)
        prod[pl.ds(pl.multiple_of(base + taps, taps), taps), :] = (
            rounded[:, c : 2 * c] * rounded[:, 2 * c :]
        ).astype(bf16)
        back[at, :] = (cot_ref[at, :].astype(f32) * rounded[:, :c]).astype(bf16)

    pair_acc[...] = jnp.zeros_like(pair_acc)
    skip_grad_ref[...] = jnp.zeros_like(skip_grad_ref)
    back_post[n:, :] = jnp.zeros((EDGE, width), bf16)
    lane_group = lax.broadcasted_iota(jnp.int32, (taps, c), 1) // per

    def pick(stacked):
        chosen = stacked[:taps]
        for g in range(1, groups):
            chosen = jnp.where(lane_group == g, stacked[g * taps : (g + 1) * taps], chosen)
        return chosen

    @pl.loop(0, blocks)
    def _(b):
        base = pl.multiple_of(b * taps, taps)
        at = pl.ds(base, taps)
        window = prod[pl.ds(base, 2 * taps), :]
        ahead = back[pl.ds(base, 2 * taps), :]
        col_pos = lax.broadcasted_iota(jnp.int32, (taps, wide), 1) + (base - taps)
        same_f = col_pos >= start_col[at, :]
        gate_f = jnp.where(same_f, 1.0, 0.0)
        row_pos = lax.broadcasted_iota(jnp.int32, (taps, wide), 0) + base
        same_b = row_pos >= start_row[:, pl.ds(base, wide)]
        gate_b = jnp.where(same_b, 1.0, 0.0).astype(bf16)
        many_f = jnp.concatenate([gate_f.astype(bf16)] * groups, axis=0)
        many_b = jnp.concatenate([gate_b] * groups, axis=0)
        conv = pick(fdot(bank_f[...] * many_f, window))
        spread = pick(fdot(bank_b[...] * many_b, ahead))
        here = ahead[:taps]
        split = jnp.concatenate(
            [jnp.where(lane_group == g, here, jnp.zeros_like(here)) for g in range(groups)], axis=0
        )
        pairs = fdot(split, window, ((1,), (1,)))
        for g in range(groups):
            span = slice(g * taps, (g + 1) * taps)
            pair_acc[span, :] += pairs[span] * gate_f
        product = window[taps:].astype(f32)
        cot = cot_ref[at, :].astype(f32)
        query = post[at, :c].astype(f32)
        key = post[at, c : 2 * c].astype(f32)
        value = post[at, 2 * c :].astype(f32)
        gated = cot * query
        skip = skip_ref[...]
        direct = conv + skip * product
        out_ref[at, :] = (query * direct).astype(bf16)
        product_back = spread + skip * gated
        skip_grad_ref[...] += jnp.sum(gated * product, axis=0, keepdims=True)
        back_post[at, :c] = (cot * direct).astype(bf16)
        back_post[at, c : 2 * c] = (product_back * value).astype(bf16)
        back_post[at, 2 * c :] = (product_back * key).astype(bf16)

    bits = taps.bit_length() - 1
    line_id = lax.broadcasted_iota(jnp.int32, (taps, wide), 0)

    @pl.loop(0, groups)
    def _(g):
        square = pair_acc[pl.ds(pl.multiple_of(g * taps, taps), taps), :]
        for bit in range(bits):
            step = 1 << bit
            square = jnp.where((line_id // step) % 2 == 1, pltpu.roll(square, wide - step, 1), square)
        long_grad_ref[pl.ds(g, 1), :] = jnp.sum(square, axis=0, keepdims=True)

    short_grad_ref[...] = jnp.zeros_like(short_grad_ref)

    @pl.loop(0, blocks)
    def _(b):
        base = pl.multiple_of(b * taps, taps)
        at = pl.ds(base, taps)
        ext = pre[pl.ds(base, taps + EDGE), :].astype(f32)
        back_ext = back_post[pl.ds(base, taps + EDGE), :].astype(f32)
        off = (
            lax.broadcasted_iota(jnp.int32, (taps + EDGE, 1), 0)
            + base
            - start_col[pl.ds(base, taps + EDGE), :]
        )
        total = jnp.zeros((taps, width), f32)
        for s in range(shorts):
            masked = back_ext * (off >= s).astype(f32)
            total = total + short_ref[s : s + 1, :] * masked[s : s + taps]
            short_grad_ref[s : s + 1, :] += jnp.sum(
                masked[:taps] * ext[EDGE - s : EDGE - s + taps], axis=0, keepdims=True
            )
        rhs[at, :width] = total.astype(bf16)

    rank = up_grad_ref.shape[0]
    back_pre = rhs[:, :width]
    up_grad_ref[...] = fdot(low_win[...], back_pre, ((0,), (0,)))[:rank]
    back_low_ref[...] = fdot(up_ref[:rank, :], back_pre, ((1,), (1,)))


def core(lengths, frozen, low, place, cot, up, short, taps_f, taps_b, skip, rank):
    n, c = cot.shape
    groups, wide = taps_f.shape
    taps = wide // 2
    kinds = frozen.shape[1]
    width = kinds * c
    f32, bf16 = jnp.float32, jnp.bfloat16
    vmem = pl.BlockSpec(memory_space=pltpu.VMEM)
    shape = jax.ShapeDtypeStruct
    return pl.pallas_call(
        core_kernel,
        out_shape=(
            shape((n, c), bf16),
            shape((rank, width), f32),
            shape((short.shape[0], width), f32),
            shape((groups, wide), f32),
            shape((1, c), f32),
            shape((rank, n), f32),
        ),
        in_specs=[pl.BlockSpec(memory_space=pltpu.SMEM)] + [vmem] * 9,
        out_specs=(vmem,) * 6,
        scratch_shapes=[
            pltpu.VMEM((n, width + LANES), bf16),
            pltpu.VMEM((n + EDGE, width), bf16),
            pltpu.VMEM((n, LANES), bf16),
            pltpu.VMEM((n, width), bf16),
            pltpu.VMEM((n + taps, c), bf16),
            pltpu.VMEM((n + taps, c), bf16),
            pltpu.VMEM((n + EDGE, width), bf16),
            pltpu.VMEM((groups * taps, wide), bf16),
            pltpu.VMEM((groups * taps, wide), bf16),
            pltpu.VMEM((groups * taps, wide), f32),
            pltpu.VMEM((n + EDGE, 1), jnp.int32),
            pltpu.VMEM((1, n + taps), jnp.int32),
        ],
        compiler_params=pltpu.CompilerParams(vmem_limit_bytes=58 * 1024 * 1024),
        cost_estimate=pl.CostEstimate(
            flops=8 * n * groups * taps * wide, bytes_accessed=16 * n * c, transcendentals=0
        ),
    )(lengths, frozen, low, place, cot, up, short, taps_f, taps_b, skip)


def by_channels(
    tokens,
    frozen,
    cotangent,
    adapter_down_weight,
    adapter_up_weight,
    short_depthwise_filter,
    long_group_filter,
    skip_direct_scale,
    document_lengths,
    window_row_position,
):
    f32, bf16 = jnp.float32, jnp.bfloat16
    rows, channels = tokens.shape
    kinds = frozen.shape[1]
    rank = adapter_down_weight.shape[0]
    shorts = short_depthwise_filter.shape[0]
    shards = lax.axis_size("ctx")
    me = lax.axis_index("ctx")
    n = rows * shards
    c = channels // shards
    taps = long_group_filter.shape[1]
    groups = long_group_filter.shape[0] // shards
    frozen_parts = frozen.reshape(rows, kinds, shards, c).transpose(2, 1, 0, 3)
    got_frozen = lax.all_to_all(frozen_parts, "ctx", split_axis=0, concat_axis=0, tiled=True)
    cot_parts = cotangent.reshape(rows, shards, c).transpose(1, 0, 2)
    got_cot = lax.all_to_all(cot_parts, "ctx", split_axis=0, concat_axis=0, tiled=True)
    part = fdot(adapter_down_weight, tokens, ((1,), (1,)))
    low_own = lax.psum(part, "tp").astype(bf16)
    place = lax.all_gather(window_row_position, "ctx", axis=0, tiled=True)
    low = lax.all_gather(low_own, "ctx", axis=0, tiled=False)
    low = low.transpose(0, 2, 1).reshape(n, rank)
    low = jnp.pad(low, ((0, 0), (0, LANES - rank)))

    def own(array):
        return lax.dynamic_slice_in_dim(array, me * c, c, array.ndim - 1)

    up = jnp.pad(own(adapter_up_weight).reshape(rank, kinds * c), ((0, LANES - rank), (0, 0)))
    short = own(short_depthwise_filter).reshape(shorts, kinds * c).astype(f32)
    skip = own(skip_direct_scale)[None, :]
    bank = lax.dynamic_slice_in_dim(long_group_filter, me * groups, groups, 0).astype(f32)
    taps_f = jnp.pad(bank[:, ::-1], ((0, 0), (1, taps - 1)))
    taps_b = jnp.pad(bank, ((0, 0), (0, taps)))
    out, up_grad, short_grad, long_line, skip_grad, back_low = core(
        document_lengths,
        got_frozen,
        low,
        place[None, :],
        got_cot.reshape(n, c),
        up,
        short,
        taps_f,
        taps_b,
        skip,
        rank,
    )
    back_low = lax.psum(back_low, ("ctx", "tp")).astype(bf16)
    out_parts = lax.all_to_all(
        out.reshape(shards, rows, c), "ctx", split_axis=0, concat_axis=0, tiled=True
    )
    mixer_out = out_parts.transpose(1, 0, 2).reshape(rows, channels)
    hot = (
        jnp.arange(n, dtype=jnp.int32)[:, None] == window_row_position[None, :]
    ).astype(bf16)
    back_own = fdot(back_low, hot).astype(bf16)
    grad_down = lax.psum(fdot(back_own, tokens), "ctx")
    long_grad = long_line[:, 1 : taps + 1][:, ::-1]
    packed = jnp.concatenate(
        [up_grad.reshape(-1), short_grad.reshape(-1), long_grad.reshape(-1), skip_grad.reshape(-1)]
    )
    packed = lax.all_gather(packed, "ctx", axis=0, tiled=False)
    cuts = [rank * kinds * c, shorts * kinds * c, groups * taps, c]
    edges = [sum(cuts[:i]) for i in range(5)]
    pieces = [packed[:, edges[i] : edges[i + 1]] for i in range(4)]

    def spread(piece, lead):
        return piece.reshape((shards,) + lead + (c,)).transpose(1, 2, 0, 3).reshape(lead + (channels,))

    return (
        mixer_out,
        grad_down,
        spread(pieces[0], (rank, kinds)),
        spread(pieces[1], (shorts, kinds)),
        pieces[2].reshape(shards * groups, taps),
        pieces[3].reshape(channels),
    )


def from_behind(value, axis, steps):
    count = lax.axis_size(axis)
    first, last = (max(0, -steps), min(count, count - steps))
    return lax.ppermute(value, axis, [(source, source + steps) for source in range(first, last)])


def doc_offsets(positions, document_lengths):
    doc_ends = jnp.cumsum(document_lengths)
    starts = doc_ends - document_lengths
    clipped = jnp.maximum(positions, 0)
    begins = jnp.max(jnp.where(starts[None, :] <= clipped[:, None], starts[None, :], 0), axis=1)
    return clipped - begins


def tap_mask(offsets, shift_tap, ndim):
    return (shift_tap <= offsets).astype(jnp.float32).reshape((-1,) + (1,) * (ndim - 1))


def pick_rows(source, row_index):
    padded = jnp.concatenate([source, jnp.zeros((1,) + source.shape[1:], source.dtype)])
    return jnp.take(padded, row_index, axis=0)


def short_apply(extended, filter_taps, offsets):
    length = offsets.shape[0]
    taps = filter_taps.shape[0]
    reach = taps - 1
    running = jnp.zeros((length,) + extended.shape[1:], jnp.float32)
    for shift_tap in range(taps):
        shifted = extended[reach - shift_tap : reach - shift_tap + length].astype(jnp.float32)
        running = running + filter_taps[shift_tap].astype(jnp.float32) * shifted * tap_mask(
            offsets, shift_tap, extended.ndim
        )
    return running


def short_back(back_ext, filter_taps, offsets_ext):
    taps = filter_taps.shape[0]
    length = back_ext.shape[0] - (taps - 1)
    running = jnp.zeros((length,) + back_ext.shape[1:], jnp.float32)
    for shift_tap in range(taps):
        shifted = back_ext[shift_tap : shift_tap + length].astype(jnp.float32)
        masked = shifted * tap_mask(
            offsets_ext[shift_tap : shift_tap + length], shift_tap, back_ext.ndim
        )
        running = running + filter_taps[shift_tap].astype(jnp.float32) * masked
    return running


def short_grad(back_post, pre_ext, offsets, taps):
    length = offsets.shape[0]
    reach = taps - 1
    back_float = back_post.astype(jnp.float32)
    collected = []
    for shift_tap in range(taps):
        shifted = pre_ext[reach - shift_tap : reach - shift_tap + length].astype(jnp.float32)
        collected.append(
            jnp.sum(back_float * shifted * tap_mask(offsets, shift_tap, pre_ext.ndim), axis=0)
        )
    return jnp.stack(collected)


def toeplitz(filter_bank):
    groups = filter_bank.shape[0]
    row_vals = jnp.concatenate(
        [
            jnp.zeros((groups, 1), filter_bank.dtype),
            filter_bank[:, ::-1],
            jnp.zeros((groups, 128), filter_bank.dtype),
        ],
        axis=1,
    )
    tiled = jnp.broadcast_to(row_vals[:, None, :], (groups, 128, 257)).reshape(groups, 128 * 257)
    return tiled[:, : 128 * 256].reshape(groups, 128, 256)


def masked_bank(filter_bank, block_off):
    row_ids = jnp.arange(128, dtype=jnp.int32)[:, None]
    col_ids = jnp.arange(256, dtype=jnp.int32)[None, :]
    allowed = (row_ids + 128 - col_ids <= block_off[:, None]).astype(filter_bank.dtype)
    return filter_bank * allowed[None]


def adapter_hidden(row_tile_block, adapter_down_weight):
    partial_low = lax.dot_general(
        adapter_down_weight,
        row_tile_block,
        (((1,), (1,)), ((), ())),
        preferred_element_type=jnp.float32,
    )
    return lax.psum(partial_low, "tp").astype(jnp.bfloat16)


def on_device(
    tokens,
    frozen,
    cotangent,
    adapter_down_weight,
    adapter_up_weight,
    short_depthwise_filter,
    long_group_filter,
    skip_direct_scale,
    document_lengths,
    window_row_position,
):
    local_rows, channels = tokens.shape
    short_count = short_depthwise_filter.shape[0]
    reach = short_count - 1
    groups = channels // 16
    blocks = local_rows // 128
    shards = lax.axis_size("ctx")
    capacity = 2 * local_rows // shards
    my_index = lax.axis_index("ctx")
    first_pos = my_index * local_rows
    all_pos = lax.all_gather(window_row_position, "ctx", axis=0, tiled=True)
    shard_ids = jnp.arange(shards, dtype=jnp.int32)
    own_dest = window_row_position // local_rows
    own_hits = (own_dest[:, None] == shard_ids[None, :]).astype(jnp.int32)
    own_rank = jnp.sum(jnp.cumsum(own_hits, axis=0) * own_hits, axis=1) - 1
    own_slot = own_dest * capacity + own_rank
    send_rows = (
        jnp.full((shards * capacity,), local_rows, jnp.int32)
        .at[own_slot]
        .set(jnp.arange(local_rows, dtype=jnp.int32))
    )
    grid_pos = all_pos.reshape(shards, local_rows)
    arriving = grid_pos // local_rows == my_index
    arrive_rank = jnp.cumsum(arriving.astype(jnp.int32), axis=1) - 1
    arrive_slot = shard_ids[:, None] * capacity + arrive_rank
    local_target = jnp.where(arriving, grid_pos % local_rows, local_rows)
    recv_rows = (
        jnp.zeros((local_rows,), jnp.int32)
        .at[local_target.reshape(-1)]
        .set(arrive_slot.reshape(-1), mode="drop")
    )
    frozen_buf = pick_rows(frozen, send_rows).reshape((shards, capacity) + frozen.shape[1:])
    token_buf = pick_rows(tokens, send_rows).reshape(shards, capacity, channels)
    got_tokens, got_frozen = (
        lax.all_to_all(token_buf, "ctx", split_axis=0, concat_axis=0, tiled=True),
        lax.all_to_all(frozen_buf, "ctx", split_axis=0, concat_axis=0, tiled=True),
    )
    packed_token_rows = jnp.take(got_tokens.reshape(shards * capacity, channels), recv_rows, axis=0)
    packed_frozen = jnp.take(
        got_frozen.reshape((shards * capacity,) + frozen.shape[1:]), recv_rows, axis=0
    )
    lowrank_product = adapter_hidden(packed_token_rows, adapter_down_weight)
    before_convolution = (
        packed_frozen.astype(jnp.float32)
        + jnp.einsum(
            "ed,ejg->djg", lowrank_product, adapter_up_weight, preferred_element_type=jnp.float32
        )
    ).astype(jnp.bfloat16)
    positions = first_pos - 127 + jnp.arange(local_rows + 255, dtype=jnp.int32)
    offsets_all = doc_offsets(positions, document_lengths)
    own_off = offsets_all[127 : 127 + local_rows]
    pre_edge = from_behind(before_convolution[-reach:], "ctx", 1)
    pre_ext = jnp.concatenate([pre_edge, before_convolution])
    post_conv = short_apply(pre_ext, short_depthwise_filter, own_off).astype(jnp.bfloat16)
    product = (post_conv[:, 1].astype(jnp.float32) * post_conv[:, 2].astype(jnp.float32)).astype(
        jnp.bfloat16
    )
    product_edge = from_behind(product[-127:], "ctx", 1)
    product_ext = jnp.concatenate([jnp.zeros((1, channels), jnp.bfloat16), product_edge, product])
    filter_bank = toeplitz(long_group_filter)
    windows = jnp.concatenate(
        [
            product_ext[:-128].reshape(blocks, 128, channels),
            product_ext[128:].reshape(blocks, 128, channels),
        ],
        axis=1,
    )
    block_offsets = own_off.reshape(blocks, 128)

    def forward_block(pieces):
        window_rows, block_off = pieces
        masked = masked_bank(filter_bank, block_off)
        return jnp.einsum(
            "gij,jgc->igc",
            masked,
            window_rows.reshape(256, groups, 16),
            preferred_element_type=jnp.float32,
        ).reshape(128, channels)

    convolved = lax.map(forward_block, (windows, block_offsets)).reshape(local_rows, channels)
    query_rows = post_conv[:, 0].astype(jnp.float32)
    key_rows = post_conv[:, 1].astype(jnp.float32)
    value_rows = post_conv[:, 2].astype(jnp.float32)
    product_float = product.astype(jnp.float32)
    direct_term = convolved + skip_direct_scale[None, :] * product_float
    mixer_out = (query_rows * direct_term).astype(jnp.bfloat16)
    grad_float = cotangent.astype(jnp.float32)
    gated_back = grad_float * query_rows
    back_conv = gated_back.astype(jnp.bfloat16)
    conv_edge = from_behind(back_conv[:127], "ctx", -1)
    edge_block = jnp.concatenate([conv_edge, jnp.zeros((1, channels), jnp.bfloat16)])

    def backward_block(pieces):
        window_rows, conv_rows, block_off = pieces
        masked = masked_bank(filter_bank, block_off)
        split_conv = conv_rows.reshape(128, groups, 16)
        spread = jnp.einsum(
            "gij,igc->jgc", masked, split_conv, preferred_element_type=jnp.float32
        ).reshape(256, channels)
        pair_sums = jnp.einsum(
            "igc,jgc->gij",
            split_conv,
            window_rows.reshape(256, groups, 16),
            preferred_element_type=jnp.float32,
        )
        skewed = jnp.pad(pair_sums.reshape(groups, 128 * 256), ((0, 0), (0, 128))).reshape(
            groups, 128, 257
        )[:, :, 1:129][:, :, ::-1]
        allowed = (jnp.arange(128, dtype=jnp.int32)[None, :] <= block_off[:, None]).astype(
            jnp.float32
        )
        return (spread, jnp.sum(skewed * allowed[None], axis=1))

    spread_all, filter_parts = lax.map(
        backward_block, (windows, back_conv.reshape(blocks, 128, channels), block_offsets)
    )
    edge_off = offsets_all[127 + local_rows : 127 + local_rows + 128]
    edge_bank = masked_bank(filter_bank, edge_off)[:, :, :128]
    edge_spread = jnp.einsum(
        "gij,igc->jgc",
        edge_bank,
        edge_block.reshape(128, groups, 16),
        preferred_element_type=jnp.float32,
    ).reshape(128, channels)
    following = jnp.concatenate([spread_all[1:, :128], edge_spread[None]], axis=0).reshape(
        local_rows, channels
    )
    product_back = (
        spread_all[:, 128:].reshape(local_rows, channels)
        + following
        + skip_direct_scale[None, :] * gated_back
    )
    grad_long = jnp.sum(filter_parts, axis=0)
    grad_skip = jnp.sum(gated_back * product_float, axis=0)
    query_back = grad_float * direct_term
    back_post = jnp.stack(
        [query_back, product_back * value_rows, product_back * key_rows], axis=1
    ).astype(jnp.bfloat16)
    post_edge = from_behind(back_post[:reach], "ctx", -1)
    back_ext = jnp.concatenate([back_post, post_edge])
    gradient_before_filter = short_back(
        back_ext, short_depthwise_filter, offsets_all[127 : 127 + local_rows + reach]
    ).astype(jnp.bfloat16)
    grad_short = short_grad(back_post, pre_ext, own_off, short_count)
    up_gradient = jnp.einsum(
        "kp,pme->kme", lowrank_product, gradient_before_filter, preferred_element_type=jnp.float32
    )
    partial_gradient = jnp.einsum(
        "ldx,idx->li", adapter_up_weight, gradient_before_filter, preferred_element_type=jnp.float32
    )
    back_low = lax.psum(partial_gradient, "tp").astype(jnp.bfloat16)
    grad_down = jnp.dot(back_low, packed_token_rows, preferred_element_type=jnp.float32)
    summed = lax.psum((grad_down, up_gradient, grad_short, grad_long, grad_skip), "ctx")
    return (mixer_out,) + tuple(summed)


def solution(mesh):
    placed = (
        P("ctx", "tp"),
        P("ctx", None, "tp"),
        P("ctx", "tp"),
        P(None, "tp"),
        P(None, None, "tp"),
        P(None, None, "tp"),
        P("tp", None),
        P("tp"),
        P(),
        P("ctx"),
    )
    channels_each = mesh.shape["ctx"] * LANES

    def run(*args):
        fits = args[0].shape[1] % channels_each == 0
        return (by_channels if fits else on_device)(*args)

    return jax.shard_map(
        run,
        mesh=mesh,
        in_specs=placed,
        out_specs=(
            P("ctx", "tp"),
            P(None, "tp"),
            P(None, None, "tp"),
            P(None, None, "tp"),
            P("tp", None),
            P("tp"),
        ),
        check_vma=False,
    )
```

profile of v0, /device:TPU:0, one launch (start us, length us, event | category | flops | bytes accessed | tf_op | source)
XLA Modules:
  0.0 265.5 jit_solution(14090240572815266082)
XLA Ops:
  7.2 2.4 copy.43
  9.5 5.2 %all-to-all-start.1 = ((bf16[8,256,256]{2,1,0:T(8,128)(2,1)}), bf16[8,256,256]{2,1,0:T(8,128)(2,1)S(1)}, u32[]{:S(2)}, u32[]{:S(2)}) async-start(bf16[8,256,256]{2,1,0:T(8,128)(2,1)} %bitcast.49), calls=%async_computation.1 | async-start | bytes 2097152 | tf_op jit(solution)/shard_map/all_to_all | solution.py:279
  14.7 4.6 %copy.28 = bf16[256,3,2048]{0,2,1:T(8,128)(2,1)} copy(bf16[256,3,2048]{2,0,1:T(8,128)(2,1)} %param.11) | data formatting | bytes 6291456 | tf_op args[1]
  19.3 4.6 %copy.29 = bf16[256,3,8,256]{3,0,1,2:T(8,128)(2,1)} copy(bf16[256,3,8,256]{0,3,2,1:T(8,128)(2,1)} %bitcast.52) | data formatting | bytes 6291456 | tf_op jit(solution)/shard_map/reshape | solution.py:276
  24.0 6.1 %all-to-all-done.1 = bf16[8,256,256]{2,1,0:T(8,128)(2,1)S(1)} async-done(((bf16[8,256,256]{2,1,0:T(8,128)(2,1)}), bf16[8,256,256]{2,1,0:T(8,128)(2,1)S(1)}, u32[]{:S(2)}, u32[]{:S(2)}) %all-to-all-start.1) | async-done | bytes 1048608 | tf_op jit(solution)/shard_map/all_to_all | solution.py:279
  30.1 1.0 copy-done.1
  31.1 4.4 %all-to-all-start = ((bf16[8,3,256,256]{3,2,1,0:T(8,128)(2,1)}), bf16[8,3,256,256]{3,2,1,0:T(8,128)(2,1)}, u32[]{:S(2)}, u32[]{:S(2)}) async-start(bf16[8,3,256,256]{3,2,1,0:T(8,128)(2,1)} %bitcast.51), calls=%async_computation | async-start | bytes 6291456 | tf_op jit(solution)/shard_map/all_to_all | solution.py:277
  35.9 19.0 %psum.21 = bf16[16,256]{1,0:T(8,128)(2,1)S(1)} all-reduce(f32[16,256]{1,0:T(8,128)S(1)} %fusion.7), channel_id=1, replica_groups=mesh['ctx'=8,'tp'=4] {'tp'}, use_global_device_ids=true, to_apply=%region_0.0 | all-reduce | flops 4096 | bytes 24576 | tf_op jit(solution)/shard_map/psum | solution.py:281
  55.0 21.8 %all-gather = bf16[128,256]{1,0:T(8,128)(2,1)S(1)} all-gather(bf16[16,256]{1,0:T(8,128)(2,1)S(1)} %psum.21), channel_id=2, replica_groups=mesh['ctx'=8,'tp'=4] {'ctx'}, dimensions={0}, use_global_device_ids=true | all-gather | bytes 73728 | tf_op jit(solution)/shard_map/all_gather | solution.py:283
  77.0 0.8 dynamic-slice_bitcast_fusion
  77.8 0.9 pad.16.low_ref
  78.7 0.7 pad.17.up_ref
  79.4 0.7 convert_bitcast_fusion
  82.7 1.3 dynamic_slice.15
  84.1 8.6 %all-gather.2 = s32[8,1,256]{2,1,0:T(1,128)} all-gather(s32[1,1,256]{2,1,0:T(1,128)S(1)} %bitcast.71), channel_id=1, replica_groups=mesh['ctx'=8,'tp'=4] {'ctx'}, dimensions={0}, use_global_device_ids=true | all-gather | bytes 9216 | tf_op jit(solution)/shard_map/all_gather | solution.py:282
  92.7 57.9 %shard_map.145 = (bf16[2048,256]{1,0:T(8,128)(2,1)}, f32[16,768]{1,0:T(8,128)}, f32[3,768]{1,0:T(4,128)}, f32[16,256]{1,0:T(8,128)}, f32[1,256]{1,0:T(1,128)}, /*index=5*/f32[16,2048]{1,0:T(8,128)}) custom-call(s32[16]{0:T(128)} %lengths_ref.1, bf16[8,3,256,256]{3,2,1,0:T(8,128)(2,1)} %all-to-all-done.frozen_ref, bf16[2048,128]{1,0:T(8,128)(2,1)} %pad.16.low_ref, ...), custom_call_target="tpu_custom_call" | custom-call | flops 8589934592 | bytes 8388608 | tf_op jit(solution)/shard_map/pallas_call | solution.py:220
  150.6 3.7 %all-to-all-start.2 = ((bf16[8,256,256]{2,1,0:T(8,128)(2,1)}), bf16[8,256,256]{2,1,0:T(8,128)(2,1)S(1)}, u32[]{:S(2)}, u32[]{:S(2)}) async-start(bf16[8,256,256]{2,1,0:T(8,128)(2,1)} %bitcast.62), calls=%async_computation.2 | async-start | bytes 2097152 | tf_op jit(solution)/shard_map/all_to_all | solution.py:310
  154.3 49.1 %all-reduce.8 = bf16[16,2048]{1,0:T(8,128)(2,1)S(1)} all-reduce(f32[16,2048]{1,0:T(8,128)} %get-tuple-element.13), channel_id=1, replica_groups=mesh['ctx'=8,'tp'=4] {'ctx','tp'}, use_global_device_ids=true, to_apply=%region_1.2 | all-reduce | flops 32768 | bytes 196608 | tf_op jit(solution)/shard_map/psum | solution.py:309
  203.5 1.5 fusion.2
  205.2 10.7 %all-gather.3 = f32[8,1,16896]{2,1,0:T(1,128)S(1)} all-gather(f32[1,1,16896]{2,1,0:T(1,128)S(1)} %reshape.89), channel_id=3, replica_groups=mesh['ctx'=8,'tp'=4] {'ctx'}, dimensions={0}, use_global_device_ids=true | all-gather | bytes 608256 | tf_op jit(solution)/shard_map/all_gather | solution.py:323
  216.1 0.8 reshape.79
  218.9 1.1 copy.38
  220.0 37.1 %all-reduce.7.cloned.1.call-done = f32[16,2048]{1,0:T(8,128)} async-done(((f32[16,2048]{1,0:T(8,128)}), f32[16,2048]{1,0:T(8,128)}) %all-reduce.7.cloned.1.call-update) | async-done | bytes 131088 | tf_op jit(solution)/shard_map/psum | solution.py:318
  257.1 1.6 copy.48
  (42 shorter events, 5.6 us)
Async XLA Ops:
  7.2 28.4 %copy-start = (bf16[256,2048]{1,0:T(8,128)(2,1)S(1)}, bf16[256,2048]{1,0:T(8,128)(2,1)}, u32[]{:S(2)}) copy-start(bf16[256,2048]{1,0:T(8,128)(2,1)} %param.10) | copy-start | bytes 3145732
  9.5 20.6 %all-to-all-start.1 = ((bf16[8,256,256]{2,1,0:T(8,128)(2,1)}), bf16[8,256,256]{2,1,0:T(8,128)(2,1)S(1)}, u32[]{:S(2)}, u32[]{:S(2)}) async-start(bf16[8,256,256]{2,1,0:T(8,128)(2,1)} %bitcast.49), calls=%async_computation.1 | async-start | bytes 2097152 | tf_op jit(solution)/shard_map/all_to_all | solution.py:279
  30.1 1.0 copy-start.1
  30.1 5.4 %copy-start.2 = (bf16[16,2048]{1,0:T(8,128)(2,1)S(1)}, bf16[16,2048]{1,0:T(8,128)(2,1)}, u32[]{:S(2)}) copy-start(bf16[16,2048]{1,0:T(8,128)(2,1)} %param.13) | copy-start | bytes 196612
  31.1 61.6 %all-to-all-start = ((bf16[8,3,256,256]{3,2,1,0:T(8,128)(2,1)}), bf16[8,3,256,256]{3,2,1,0:T(8,128)(2,1)}, u32[]{:S(2)}, u32[]{:S(2)}) async-start(bf16[8,3,256,256]{3,2,1,0:T(8,128)(2,1)} %bitcast.51), calls=%async_computation | async-start | bytes 6291456 | tf_op jit(solution)/shard_map/all_to_all | solution.py:277
  35.5 48.5 %copy-start.6 = (s32[256]{0:T(256)S(1)}, s32[256]{0:T(256)}, u32[]{:S(2)}) copy-start(s32[256]{0:T(256)} %param.19) | copy-start | bytes 3076
  150.6 54.4 %copy-start.5 = (f32[16,256]{1,0:T(8,128)S(1)}, f32[16,256]{1,0:T(8,128)}, u32[]{:S(2)}) copy-start(f32[16,256]{1,0:T(8,128)} %get-tuple-element.16) | copy-start | bytes 49156
  150.6 54.6 %copy-start.4 = (f32[3,768]{1,0:T(4,128)S(1)}, f32[3,768]{1,0:T(4,128)}, u32[]{:S(2)}) copy-start(f32[3,768]{1,0:T(4,128)} %get-tuple-element.15) | copy-start | bytes 27652
  150.6 54.6 %copy-start.3 = (f32[16,768]{1,0:T(8,128)S(1)}, f32[16,768]{1,0:T(8,128)}, u32[]{:S(2)}) copy-start(f32[16,768]{1,0:T(8,128)} %get-tuple-element.14) | copy-start | bytes 147460
  150.6 54.6 %copy-start.7 = (f32[1,256]{1,0:T(1,128)S(1)}, f32[1,256]{1,0:T(1,128)}, u32[]{:S(2)}) copy-start(f32[1,256]{1,0:T(1,128)} %get-tuple-element.17) | copy-start | bytes 3076
  150.6 68.3 %all-to-all-start.2 = ((bf16[8,256,256]{2,1,0:T(8,128)(2,1)}), bf16[8,256,256]{2,1,0:T(8,128)(2,1)S(1)}, u32[]{:S(2)}, u32[]{:S(2)}) async-start(bf16[8,256,256]{2,1,0:T(8,128)(2,1)} %bitcast.62), calls=%async_computation.2 | async-start | bytes 2097152 | tf_op jit(solution)/shard_map/all_to_all | solution.py:310
  154.3 102.8 %all-reduce.7.cloned.1.call-start = ((), (), s32[]{:S(2)}) async-start(), calls=%async_computation.3 | async-start | bytes 262144 | tf_op jit(solution)/shard_map/psum | solution.py:318
Sparse Core Ops, SparseCore 0:
  205.1 51.9 all-reduce.6
where the time goes:
time: 266 us; the launch traced here: 265 us
  blocking collectives  109 us (41%)
  Pallas kernels  57.9 us (22%)
  waiting for transfers between devices  43.3 us (16%)
  local copies, waits for them, and re-layouts  24.3 us (9%)
  between operations  14.2 us (5%)
  starting transfers between devices  13.3 us (5%)
    pallas_call x1, Pallas kernels, core(): pl.pallas_call(core_kernel, out_shape=(shape((n, c), bf16), shape((rank,...  57.9 us
    psum x1, blocking collectives, by_channels(): back_low = lax.psum(back_low, ('ctx', 'tp')).astype(bf16)  49.1 us
    psum x1, waiting for transfers between devices, by_channels(): grad_down = lax.psum(fdot(back_own, tokens), 'ctx')  37.1 us
    all_gather x1, blocking collectives, by_channels(): low = lax.all_gather(low_own, 'ctx', axis=0, tiled=False)  21.8 us
    psum x1, blocking collectives, by_channels(): low_own = lax.psum(part, 'tp').astype(bf16)  19 us
    all_gather x1, blocking collectives, by_channels(): packed = lax.all_gather(packed, 'ctx', axis=0, tiled=False)  10.7 us
    unnamed x24, local copies, waits for them, and re-layouts  9.26 us
    all_gather x1, blocking collectives, by_channels(): place = lax.all_gather(window_row_position, 'ctx', axis=0, tiled=True)  8.65 us
  transfers between devices with their start and end apart: 4, of which 2 were waited for; matrix products, arithmetic and copies ran while one was open for 9% of the time, Pallas kernels for 0%

commit v1 on v0

--- a/solution.py
+++ b/solution.py
@@ -24,23 +24,80 @@
     return begins
 
 
-def core_kernel(
+def ctx_peers():
+    me, count = lax.axis_index("ctx"), lax.axis_size("ctx")
+    return me, [(d, lax.rem(me + d, count)) for d in range(1, count)]
+
+
+def tp_peers():
+    me, count = lax.axis_index("tp"), lax.axis_size("tp")
+    return me, [(d, lax.rem(me + d, count)) for d in range(1, count)]
+
+
+def greet():
+    barrier = pltpu.get_barrier_semaphore()
+    waits = 0
+    for axis, (_, peers) in (("ctx", ctx_peers()), ("tp", tp_peers())):
+        for _, peer in peers:
+            pl.semaphore_signal(
+                barrier, inc=1, device_id={axis: peer}, device_id_type=pl.DeviceIdType.MESH
+            )
+            waits += 1
+    pl.semaphore_wait(barrier, waits)
+
+
+def push(src, dst, send_sem, recv_sem, axis, peer):
+    copy = pltpu.make_async_remote_copy(
+        src_ref=src,
+        dst_ref=dst,
+        send_sem=send_sem,
+        recv_sem=recv_sem,
+        device_id={axis: peer},
+        device_id_type=pl.DeviceIdType.MESH,
+    )
+    copy.start()
+    return copy
+
+
+def part_of(index, size):
+    return pl.ds(pl.multiple_of(index * size, size), size)
+
+
+def mixer_kernel(
     lengths_ref,
     frozen_ref,
-    low_ref,
-    place_ref,
-    cot_ref,
+    cot_in_ref,
+    tokens_ref,
+    down_ref,
+    pos_ref,
     up_ref,
     short_ref,
     taps_f_ref,
     taps_b_ref,
     skip_ref,
+    mixer_out,
+    grad_down,
+    grad_up,
+    grad_small,
+    grad_long,
+    got_frozen,
+    cot_ref,
+    low_all,
+    place_all,
     out_ref,
     up_grad_ref,
     short_grad_ref,
     long_grad_ref,
-    skip_grad_ref,
     back_low_ref,
+    low_got,
+    back_parts,
+    back_own_low,
+    back_all,
+    down_part,
+    down_got,
+    down_own,
+    low_parts,
+    low_own,
     rhs,
     pre,
     low_win,
@@ -53,16 +110,72 @@
     pair_acc,
     start_col,
     start_row,
+    send_sems,
+    recv_sems,
+    own_sems,
+    tp_send,
+    tp_recv,
 ):
     n, c = cot_ref.shape
     groups, wide = taps_f_ref.shape
     taps = wide // 2
     per = c // groups
-    shards, kinds, rows, _ = frozen_ref.shape
+    shards, kinds, rows, _ = got_frozen.shape
     width = kinds * c
     blocks = n // taps
     shorts = short_ref.shape[0]
+    rank = down_ref.shape[0]
     f32, bf16 = jnp.float32, jnp.bfloat16
+    me, peers = ctx_peers()
+    tp_me, tp_others = tp_peers()
+    mine, my_rows = part_of(me, c), part_of(me, rows)
+    greet()
+
+    def everyone(step, source, target):
+        return [
+            push(source(peer), target, send_sems.at[step, d], recv_sems.at[step, d], "ctx", peer)
+            for d, peer in peers
+        ]
+
+    def tp_swap(step, parts):
+        return [
+            push(
+                parts.at[tp_me],
+                parts.at[tp_me],
+                tp_send.at[step, d],
+                tp_recv.at[step, d],
+                "tp",
+                peer,
+            )
+            for d, peer in tp_others
+        ]
+
+    def finish(copies):
+        for copy in copies:
+            copy.wait()
+
+    def tidy(parts, count):
+        total = parts[0]
+        for t in range(1, count):
+            total = total + parts[t]
+        return total
+
+    places = everyone(8, lambda peer: pos_ref, place_all.at[me])
+    frozens = everyone(
+        9, lambda peer: frozen_ref.at[:, :, part_of(peer, c)], got_frozen.at[me]
+    )
+    own_frozen = pltpu.make_async_copy(frozen_ref.at[:, :, mine], got_frozen.at[me], own_sems.at[0])
+    own_frozen.start()
+    own_cot = pltpu.make_async_copy(cot_in_ref.at[:, mine], cot_ref.at[my_rows], own_sems.at[1])
+    own_cot.start()
+    place_all[me] = pos_ref[...]
+    low_parts[tp_me] = fdot(down_ref[...], tokens_ref[...], ((1,), (1,)))
+    swaps = tp_swap(0, low_parts)
+    cots = everyone(10, lambda peer: cot_in_ref.at[:, part_of(peer, c)], cot_ref.at[my_rows])
+    finish(swaps)
+    low_own[...] = tidy(low_parts, low_parts.shape[0]).astype(bf16)
+    low_all[me] = low_own[...]
+    lows = everyone(11, lambda peer: low_own, low_all.at[me])
 
     start_col[...] = doc_starts(
         lax.broadcasted_iota(jnp.int32, start_col.shape, 0), lengths_ref
@@ -77,13 +190,26 @@
             line = jnp.broadcast_to(taps_ref[g : g + 1, :], (taps, wide))
             bank[span, :] = pltpu.roll(line, 0, 1, stride=1, stride_axis=0).astype(bf16)
 
-    @pl.loop(0, shards)
-    def _(j):
-        at = pl.ds(pl.multiple_of(j * rows, rows), rows)
-        low = low_ref[at, :]
+    unit = jnp.where(
+        lax.broadcasted_iota(jnp.int32, (rank, LANES), 0)
+        == lax.broadcasted_iota(jnp.int32, (rank, LANES), 1),
+        1.0,
+        0.0,
+    ).astype(bf16)
+
+    finish(places)
+    finish(lows)
+    for d in range(shards):
+        if d == 0:
+            own_frozen.wait()
+        else:
+            frozens[d - 1].wait()
+        j = lax.rem(me + shards - d, shards)
+        at = part_of(j, rows)
+        low = fdot(low_all[j], unit, ((0,), (0,))).astype(bf16)
         for a in range(kinds):
             cols = slice(a * c, (a + 1) * c)
-            rhs[at, cols] = (frozen_ref[j, a].astype(f32) + fdot(low, up_ref[:, cols])).astype(bf16)
+            rhs[at, cols] = (got_frozen[j, a].astype(f32) + fdot(low, up_ref[:, cols])).astype(bf16)
         rhs[at, width:] = low
 
     pre[:EDGE, :] = jnp.zeros((EDGE, width), bf16)
@@ -92,12 +218,16 @@
     @pl.loop(0, n // tall)
     def _(w):
         base = pl.multiple_of(w * tall, tall)
-        spot = lax.broadcasted_iota(jnp.int32, (tall, n), 0) + base
-        hot = jnp.where(place_ref[...] == spot, 1.0, 0.0).astype(bf16)
+        spot = lax.broadcasted_iota(jnp.int32, (tall, rows), 0) + base
+        hot = jnp.concatenate(
+            [jnp.where(place_all[j] == spot, 1.0, 0.0).astype(bf16) for j in range(shards)], axis=1
+        )
         moved = fdot(hot, rhs[...]).astype(bf16)
         pre[pl.ds(pl.multiple_of(base + EDGE, EDGE), tall), :] = moved[:, :width]
         low_win[pl.ds(base, tall), :] = moved[:, width:]
 
+    own_cot.wait()
+    finish(cots)
     prod[:taps, :] = jnp.zeros((taps, c), bf16)
     back[n:, :] = jnp.zeros((taps, c), bf16)
 
@@ -120,9 +250,18 @@
         back[at, :] = (cot_ref[at, :].astype(f32) * rounded[:, :c]).astype(bf16)
 
     pair_acc[...] = jnp.zeros_like(pair_acc)
-    skip_grad_ref[...] = jnp.zeros_like(skip_grad_ref)
+    short_grad_ref[...] = jnp.zeros_like(short_grad_ref)
     back_post[n:, :] = jnp.zeros((EDGE, width), bf16)
     lane_group = lax.broadcasted_iota(jnp.int32, (taps, c), 1) // per
+
+    turned = wide - 1 - lax.broadcasted_iota(jnp.int32, (taps, wide), 1)
+    flip = jnp.where(
+        lax.broadcasted_iota(jnp.int32, (wide, wide), 0)
+        + lax.broadcasted_iota(jnp.int32, (wide, wide), 1)
+        == wide - 1,
+        1.0,
+        0.0,
+    ).astype(bf16)
 
     def pick(stacked):
         chosen = stacked[:taps]
@@ -138,11 +277,12 @@
         ahead = back[pl.ds(base, 2 * taps), :]
         col_pos = lax.broadcasted_iota(jnp.int32, (taps, wide), 1) + (base - taps)
         same_f = col_pos >= start_col[at, :]
-        gate_f = jnp.where(same_f, 1.0, 0.0)
+        gate_f = jnp.where(same_f, 1.0, 0.0).astype(bf16)
+        gate_r = jnp.where(turned + (base - taps) >= start_col[at, :], 1.0, 0.0)
         row_pos = lax.broadcasted_iota(jnp.int32, (taps, wide), 0) + base
         same_b = row_pos >= start_row[:, pl.ds(base, wide)]
         gate_b = jnp.where(same_b, 1.0, 0.0).astype(bf16)
-        many_f = jnp.concatenate([gate_f.astype(bf16)] * groups, axis=0)
+        many_f = jnp.concatenate([gate_f] * groups, axis=0)
         many_b = jnp.concatenate([gate_b] * groups, axis=0)
         conv = pick(fdot(bank_f[...] * many_f, window))
         spread = pick(fdot(bank_b[...] * many_b, ahead))
@@ -150,10 +290,10 @@
         split = jnp.concatenate(
             [jnp.where(lane_group == g, here, jnp.zeros_like(here)) for g in range(groups)], axis=0
         )
-        pairs = fdot(split, window, ((1,), (1,)))
+        pairs = fdot(split, fdot(flip, window).astype(bf16), ((1,), (1,)))
         for g in range(groups):
             span = slice(g * taps, (g + 1) * taps)
-            pair_acc[span, :] += pairs[span] * gate_f
+            pair_acc[span, :] += pairs[span] * gate_r
         product = window[taps:].astype(f32)
         cot = cot_ref[at, :].astype(f32)
         query = post[at, :c].astype(f32)
@@ -164,23 +304,18 @@
         direct = conv + skip * product
         out_ref[at, :] = (query * direct).astype(bf16)
         product_back = spread + skip * gated
-        skip_grad_ref[...] += jnp.sum(gated * product, axis=0, keepdims=True)
+        short_grad_ref[shorts : shorts + 1, :c] += jnp.sum(gated * product, axis=0, keepdims=True)
         back_post[at, :c] = (cot * direct).astype(bf16)
         back_post[at, c : 2 * c] = (product_back * value).astype(bf16)
         back_post[at, 2 * c :] = (product_back * key).astype(bf16)
 
-    bits = taps.bit_length() - 1
-    line_id = lax.broadcasted_iota(jnp.int32, (taps, wide), 0)
-
-    @pl.loop(0, groups)
-    def _(g):
-        square = pair_acc[pl.ds(pl.multiple_of(g * taps, taps), taps), :]
-        for bit in range(bits):
-            step = 1 << bit
-            square = jnp.where((line_id // step) % 2 == 1, pltpu.roll(square, wide - step, 1), square)
-        long_grad_ref[pl.ds(g, 1), :] = jnp.sum(square, axis=0, keepdims=True)
-
-    short_grad_ref[...] = jnp.zeros_like(short_grad_ref)
+    copies = everyone(1, lambda peer: out_ref.at[part_of(peer, rows)], mixer_out.at[:, mine])
+    own = [pltpu.make_async_copy(out_ref.at[my_rows], mixer_out.at[:, mine], own_sems.at[0])]
+    own[0].start()
+    for g in range(groups):
+        span = slice(g * taps, (g + 1) * taps)
+        square = pltpu.roll(pair_acc[span, :], wide - taps + 1, 1, stride=1, stride_axis=0)
+        long_grad_ref[g : g + 1, :] = jnp.sum(square[:, :taps], axis=0, keepdims=True)
 
     @pl.loop(0, blocks)
     def _(b):
@@ -202,34 +337,97 @@
             )
         rhs[at, :width] = total.astype(bf16)
 
-    rank = up_grad_ref.shape[0]
     back_pre = rhs[:, :width]
-    up_grad_ref[...] = fdot(low_win[...], back_pre, ((0,), (0,)))[:rank]
+    up_grad = fdot(low_win[...], back_pre, ((0,), (0,)))
+    for a in range(kinds):
+        up_grad_ref[a] = up_grad[:rank, a * c : (a + 1) * c]
     back_low_ref[...] = fdot(up_ref[:rank, :], back_pre, ((1,), (1,)))
-
-
-def core(lengths, frozen, low, place, cot, up, short, taps_f, taps_b, skip, rank):
-    n, c = cot.shape
+    reduce_low = everyone(0, lambda peer: back_low_ref.at[:, part_of(peer, rows)], low_got.at[me])
+    low_got[me] = back_low_ref[:, my_rows]
+    copies += everyone(2, lambda peer: up_grad_ref, grad_up.at[:, :, mine])
+    copies += everyone(3, lambda peer: short_grad_ref, grad_small.at[me])
+    copies += everyone(4, lambda peer: long_grad_ref, grad_long.at[part_of(me, groups)])
+    own += [
+        pltpu.make_async_copy(up_grad_ref, grad_up.at[:, :, mine], own_sems.at[1]),
+        pltpu.make_async_copy(short_grad_ref, grad_small.at[me], own_sems.at[2]),
+        pltpu.make_async_copy(long_grad_ref, grad_long.at[part_of(me, groups)], own_sems.at[3]),
+    ]
+    for copy in own[1:]:
+        copy.start()
+    finish(reduce_low)
+    total = low_got[0]
+    for j in range(1, shards):
+        total = total + low_got[j]
+    back_parts[tp_me] = total
+    finish(tp_swap(1, back_parts))
+    total = back_parts[0]
+    for t in range(1, back_parts.shape[0]):
+        total = total + back_parts[t]
+    back_own_low[...] = total.astype(bf16)
+    spread = everyone(5, lambda peer: back_own_low, back_all.at[me])
+    back_all[me] = total.astype(bf16)
+    finish(spread)
+    back_own = jnp.zeros((rank, rows), jnp.float32)
+    for j in range(shards):
+        spot = lax.broadcasted_iota(jnp.int32, (rows, rows), 0) + j * rows
+        hot = jnp.where(pos_ref[...] == spot, 1.0, 0.0).astype(bf16)
+        back_own = back_own + fdot(back_all[j], hot)
+    down_part[...] = fdot(back_own.astype(bf16), tokens_ref[...])
+    reduce_down = everyone(6, lambda peer: down_part.at[:, part_of(peer, c)], down_got.at[me])
+    down_got[me] = down_part[:, mine]
+    finish(reduce_down)
+    total = down_got[0]
+    for j in range(1, shards):
+        total = total + down_got[j]
+    down_own[...] = total
+    copies += everyone(7, lambda peer: down_own, grad_down.at[:, mine])
+    last = pltpu.make_async_copy(down_own, grad_down.at[:, mine], own_sems.at[4])
+    last.start()
+    finish(copies + own + [last])
+
+
+def mixer(lengths, frozen, cot, tokens, down, pos, up, short, taps_f, taps_b, skip):
+    kinds, rows, channels = frozen.shape
+    shards, tps = lax.axis_size("ctx"), lax.axis_size("tp")
+    n, c = rows * shards, channels // shards
     groups, wide = taps_f.shape
     taps = wide // 2
-    kinds = frozen.shape[1]
     width = kinds * c
-    f32, bf16 = jnp.float32, jnp.bfloat16
-    vmem = pl.BlockSpec(memory_space=pltpu.VMEM)
+    rank = down.shape[0]
+    small = -(-(short.shape[0] + 1) // 8) * 8
+    f32, bf16, i32 = jnp.float32, jnp.bfloat16, jnp.int32
     shape = jax.ShapeDtypeStruct
+    vmem, hbm = pl.BlockSpec(memory_space=pltpu.VMEM), pl.BlockSpec(memory_space=pl.ANY)
     return pl.pallas_call(
-        core_kernel,
+        mixer_kernel,
         out_shape=(
-            shape((n, c), bf16),
-            shape((rank, width), f32),
-            shape((short.shape[0], width), f32),
-            shape((groups, wide), f32),
-            shape((1, c), f32),
-            shape((rank, n), f32),
+            shape((rows, channels), bf16),
+            shape((rank, channels), f32),
+            shape((kinds, rank, channels), f32),
+            shape((shards, small, width), f32),
+            shape((shards * groups, taps), f32),
         ),
-        in_specs=[pl.BlockSpec(memory_space=pltpu.SMEM)] + [vmem] * 9,
-        out_specs=(vmem,) * 6,
+        in_specs=[pl.BlockSpec(memory_space=pltpu.SMEM), hbm, hbm] + [vmem] * 8,
+        out_specs=(hbm,) * 5,
         scratch_shapes=[
+            pltpu.VMEM((shards, kinds, rows, c), bf16),
+            pltpu.VMEM((n, c), bf16),
+            pltpu.VMEM((shards, rank, rows), bf16),
+            pltpu.VMEM((shards, 1, rows), i32),
+            pltpu.VMEM((n, c), bf16),
+            pltpu.VMEM((kinds, rank, c), f32),
+            pltpu.VMEM((small, width), f32),
+            pltpu.VMEM((groups, taps), f32),
+            pltpu.VMEM((rank, n), f32),
+            pltpu.VMEM((shards, rank, rows), f32),
+            pltpu.VMEM((tps, rank, rows), f32),
+            pltpu.VMEM((rank, rows), bf16),
+            pltpu.VMEM((shards, rank, rows), bf16),
+            pltpu.VMEM((rank, channels), f32),
+            pltpu.VMEM((shards, rank, c), f32),
+            pltpu.VMEM((rank, c), f32),
+            pltpu.VMEM((tps, rank, rows), f32),
+            pltpu.VMEM((rank, rows), bf16),
             pltpu.VMEM((n, width + LANES), bf16),
             pltpu.VMEM((n + EDGE, width), bf16),
             pltpu.VMEM((n, LANES), bf16),
@@ -240,14 +438,21 @@
             pltpu.VMEM((groups * taps, wide), bf16),
             pltpu.VMEM((groups * taps, wide), bf16),
             pltpu.VMEM((groups * taps, wide), f32),
-            pltpu.VMEM((n + EDGE, 1), jnp.int32),
-            pltpu.VMEM((1, n + taps), jnp.int32),
+            pltpu.VMEM((n + EDGE, 1), i32),
+            pltpu.VMEM((1, n + taps), i32),
+            pltpu.SemaphoreType.DMA((12, shards)),
+            pltpu.SemaphoreType.DMA((12, shards)),
+            pltpu.SemaphoreType.DMA((5,)),
+            pltpu.SemaphoreType.DMA((2, tps)),
+            pltpu.SemaphoreType.DMA((2, tps)),
         ],
-        compiler_params=pltpu.CompilerParams(vmem_limit_bytes=58 * 1024 * 1024),
+        compiler_params=pltpu.CompilerParams(
+            collective_id=0, has_side_effects=True, vmem_limit_bytes=58 * 1024 * 1024
+        ),
         cost_estimate=pl.CostEstimate(
             flops=8 * n * groups * taps * wide, bytes_accessed=16 * n * c, transcendentals=0
         ),
-    )(lengths, frozen, low, place, cot, up, short, taps_f, taps_b, skip)
+    )(lengths, frozen, cot, tokens, down, pos, up, short, taps_f, taps_b, skip)
 
 
 def by_channels(
@@ -273,17 +478,7 @@
     c = channels // shards
     taps = long_group_filter.shape[1]
     groups = long_group_filter.shape[0] // shards
-    frozen_parts = frozen.reshape(rows, kinds, shards, c).transpose(2, 1, 0, 3)
-    got_frozen = lax.all_to_all(frozen_parts, "ctx", split_axis=0, concat_axis=0, tiled=True)
-    cot_parts = cotangent.reshape(rows, shards, c).transpose(1, 0, 2)
-    got_cot = lax.all_to_all(cot_parts, "ctx", split_axis=0, concat_axis=0, tiled=True)
-    part = fdot(adapter_down_weight, tokens, ((1,), (1,)))
-    low_own = lax.psum(part, "tp").astype(bf16)
-    place = lax.all_gather(window_row_position, "ctx", axis=0, tiled=True)
-    low = lax.all_gather(low_own, "ctx", axis=0, tiled=False)
-    low = low.transpose(0, 2, 1).reshape(n, rank)
-    low = jnp.pad(low, ((0, 0), (0, LANES - rank)))
-
+    pos = window_row_position[None, :]
     def own(array):
         return lax.dynamic_slice_in_dim(array, me * c, c, array.ndim - 1)
 
@@ -293,48 +488,27 @@
     bank = lax.dynamic_slice_in_dim(long_group_filter, me * groups, groups, 0).astype(f32)
     taps_f = jnp.pad(bank[:, ::-1], ((0, 0), (1, taps - 1)))
     taps_b = jnp.pad(bank, ((0, 0), (0, taps)))
-    out, up_grad, short_grad, long_line, skip_grad, back_low = core(
+    mixer_out, grad_down, grad_up, grad_small, grad_long = mixer(
         document_lengths,
-        got_frozen,
-        low,
-        place[None, :],
-        got_cot.reshape(n, c),
+        frozen.transpose(1, 0, 2),
+        cotangent,
+        tokens,
+        adapter_down_weight,
+        pos,
         up,
         short,
         taps_f,
         taps_b,
         skip,
-        rank,
-    )
-    back_low = lax.psum(back_low, ("ctx", "tp")).astype(bf16)
-    out_parts = lax.all_to_all(
-        out.reshape(shards, rows, c), "ctx", split_axis=0, concat_axis=0, tiled=True
-    )
-    mixer_out = out_parts.transpose(1, 0, 2).reshape(rows, channels)
-    hot = (
-        jnp.arange(n, dtype=jnp.int32)[:, None] == window_row_position[None, :]
-    ).astype(bf16)
-    back_own = fdot(back_low, hot).astype(bf16)
-    grad_down = lax.psum(fdot(back_own, tokens), "ctx")
-    long_grad = long_line[:, 1 : taps + 1][:, ::-1]
-    packed = jnp.concatenate(
-        [up_grad.reshape(-1), short_grad.reshape(-1), long_grad.reshape(-1), skip_grad.reshape(-1)]
-    )
-    packed = lax.all_gather(packed, "ctx", axis=0, tiled=False)
-    cuts = [rank * kinds * c, shorts * kinds * c, groups * taps, c]
-    edges = [sum(cuts[:i]) for i in range(5)]
-    pieces = [packed[:, edges[i] : edges[i + 1]] for i in range(4)]
-
-    def spread(piece, lead):
-        return piece.reshape((shards,) + lead + (c,)).transpose(1, 2, 0, 3).reshape(lead + (channels,))
-
+    )
+    grad_short = grad_small[:, :shorts].reshape(shards, shorts, kinds, c).transpose(1, 2, 0, 3)
     return (
         mixer_out,
         grad_down,
-        spread(pieces[0], (rank, kinds)),
-        spread(pieces[1], (shorts, kinds)),
-        pieces[2].reshape(shards * groups, taps),
-        pieces[3].reshape(channels),
+        grad_up.transpose(1, 0, 2),
+        grad_short.reshape(shorts, kinds, channels),
+        grad_long,
+        grad_small[:, shorts, :c].reshape(channels),
     )
 
 

time: 266 us -> 149 us (0.56)
  blocking collectives: 109 us -> 0 us
  Pallas kernels: 57.9 us -> 133 us
  waiting for transfers between devices: 43.3 us -> 0 us
  between operations: 14.2 us -> 0.69 us
  starting transfers between devices: 13.3 us -> 0 us
  local copies, waits for them, and re-layouts: 24.3 us -> 13.3 us
    pallas_call x1, Pallas kernels: 57.9 us -> 133 us  [mixer(): pl.pallas_call(mixer_kernel, out_shape=(shape((rows, channels), bf16), sh...]
    psum x2 -> x0, blocking collectives: 68.1 us -> none  [the longest x1 49.1 us: by_channels(): back_low = lax.psum(back_low, ('ctx', 'tp')).astype(bf16)]
    all_gather x3 -> x0, blocking collectives: 41.2 us -> none  [the longest x1 21.8 us: by_channels(): low = lax.all_gather(low_own, 'ctx', axis=0, tiled=False)]
    psum x1 -> x0, waiting for transfers between devices: 37.1 us -> none  [by_channels(): grad_down = lax.psum(fdot(back_own, tokens), 'ctx')]
    all_to_all x3 -> x0, starting transfers between devices: 13.3 us -> none  [the longest x1 5.17 us: by_channels(): lax.all_to_all(cot_parts, 'ctx', split_axis=0, concat_axis=0, tiled=True)]
    reshape x8 -> x1, local copies, waits for them, and re-layouts: 10.2 us -> 0.68 us  [by_channels(): grad_small[:, :shorts].reshape(shards, shorts, kinds, c)]
    all_to_all x3 -> x0, waiting for transfers between devices: 6.14 us -> none  [the longest x1 6.13 us: by_channels(): lax.all_to_all(cot_parts, 'ctx', split_axis=0, concat_axis=0, tiled=True)]
    unnamed x24 -> x12, local copies, waits for them, and re-layouts: 9.26 us -> 6.78 us
  transfers between devices with their start and end apart: 4 -> 0, of which waited for: 2 -> 0; matrix products, arithmetic and copies ran while one was open for 9% -> 0% of each run, Pallas kernels for 0% -> 0%
where the time goes in v1:
time: 149 us; the launch traced here: 148 us
  Pallas kernels  133 us (89%)
  local copies, waits for them, and re-layouts  13.3 us (9%)
    pallas_call x1, Pallas kernels, mixer(): pl.pallas_call(mixer_kernel, out_shape=(shape((rows, channels), bf16), sh...  133 us
    unnamed x12, local copies, waits for them, and re-layouts  6.78 us

profile of v1, /device:TPU:0, one launch (start us, length us, event | category | flops | bytes accessed | tf_op | source)
XLA Modules:
  0.0 148.3 jit_solution(8338082328549474549)
XLA Ops:
  0.6 0.0 copy-start
  0.7 0.9 copy-done
  1.6 0.7 pad.12.up_ref
  2.3 0.7 convert_bitcast_fusion
  3.0 0.6 copy.21
  3.6 1.3 dynamic_slice.15
  4.9 0.7 dynamic-slice_convert_fusion
  5.6 0.1 rev.3
  5.7 0.7 pad.13.taps_f_ref
  6.3 0.6 pad.14.taps_b_ref
  6.9 132.9 %shard_map.145 = (bf16[256,2048]{1,0:T(8,128)(2,1)}, f32[16,2048]{1,0:T(8,128)}, f32[3,16,2048]{2,1,0:T(8,128)}, f32[8,8,768]{2,1,0:T(8,128)}, f32[128,128]{1,0:T(8,128)}) custom-call(s32[16]{0:T(128)} %lengths_ref.1, bf16[3,256,2048]{2,1,0:T(8,128)(2,1)} %bitcast.22, bf16[256,2048]{1,0:T(8,128)(2,1)} %cot_in_ref.1, bf16[256,2048]{1,0:T(8,128)(2,1)} %tokens_ref.1, ...), custom_call_target="tpu_custom_call" | custom-call | flops 8589934592 | bytes 8388608 | tf_op jit(solution)/shard_map/pallas_call | solution.py:401
  139.9 0.0 copy-start.1
  139.9 0.0 copy-start.2
  139.9 1.0 slice.6
  140.9 0.7 reshape.25
  141.6 1.4 slice.7
  143.1 2.3 %copy.26 = bf16[256,2048]{1,0:T(8,128)(2,1)} copy(bf16[256,2048]{1,0:T(8,128)(2,1)} %get-tuple-element.22) | data formatting | bytes 2097152
  145.4 1.6 %copy.27 = f32[16,2048]{1,0:T(8,128)} copy(f32[16,2048]{1,0:T(8,128)} %get-tuple-element.23) | data formatting | bytes 262144
  146.9 0.0 copy-done.1
  146.9 0.7 copy.28
  147.7 0.0 copy-done.2
  147.7 0.6 copy.29
  (3 shorter events, 0.0 us)
Async XLA Ops:
  0.6 0.9 copy-start
  139.9 7.0 %copy-start.1 = (f32[3,16,2048]{2,1,0:T(8,128)S(1)}, f32[3,16,2048]{2,1,0:T(8,128)}, u32[]{:S(2)}) copy-start(f32[3,16,2048]{2,1,0:T(8,128)} %get-tuple-element.13) | copy-start | bytes 1179652
  139.9 7.8 %copy-start.2 = (f32[128,128]{1,0:T(8,128)S(1)}, f32[128,128]{1,0:T(8,128)}, u32[]{:S(2)}) copy-start(f32[128,128]{1,0:T(8,128)} %get-tuple-element.26) | copy-start | bytes 196612

commit v2 on v1

--- a/solution.py
+++ b/solution.py
@@ -72,8 +72,7 @@
     pos_ref,
     up_ref,
     short_ref,
-    taps_f_ref,
-    taps_b_ref,
+    filter_ref,
     skip_ref,
     mixer_out,
     grad_down,
@@ -81,14 +80,14 @@
     grad_small,
     grad_long,
     got_frozen,
-    cot_ref,
+    got_cot,
     low_all,
     place_all,
-    out_ref,
-    up_grad_ref,
-    short_grad_ref,
-    long_grad_ref,
-    back_low_ref,
+    out_buf,
+    up_own,
+    small_own,
+    long_own,
+    back_low,
     low_got,
     back_parts,
     back_own_low,
@@ -98,6 +97,7 @@
     down_own,
     low_parts,
     low_own,
+    hot_ref,
     rhs,
     pre,
     low_win,
@@ -105,6 +105,8 @@
     prod,
     back,
     back_post,
+    taps_f,
+    taps_b,
     bank_f,
     bank_b,
     pair_acc,
@@ -116,14 +118,15 @@
     tp_send,
     tp_recv,
 ):
-    n, c = cot_ref.shape
-    groups, wide = taps_f_ref.shape
+    slabs, shards, kinds, rows, lanes = got_frozen.shape
+    n, c = rows * shards, lanes * slabs
+    groups, wide = taps_f.shape
     taps = wide // 2
     per = c // groups
-    shards, kinds, rows, _ = got_frozen.shape
-    width = kinds * c
+    some = groups // slabs
+    width = kinds * lanes
     blocks = n // taps
-    shorts = short_ref.shape[0]
+    shorts = short_ref.shape[0] // kinds
     rank = down_ref.shape[0]
     f32, bf16 = jnp.float32, jnp.bfloat16
     me, peers = ctx_peers()
@@ -150,6 +153,11 @@
             for d, peer in tp_others
         ]
 
+    def keep(step, source, target):
+        copy = pltpu.make_async_copy(source, target, own_sems.at[step])
+        copy.start()
+        return copy
+
     def finish(copies):
         for copy in copies:
             copy.wait()
@@ -160,100 +168,75 @@
             total = total + parts[t]
         return total
 
-    places = everyone(8, lambda peer: pos_ref, place_all.at[me])
-    frozens = everyone(
-        9, lambda peer: frozen_ref.at[:, :, part_of(peer, c)], got_frozen.at[me]
-    )
-    own_frozen = pltpu.make_async_copy(frozen_ref.at[:, :, mine], got_frozen.at[me], own_sems.at[0])
-    own_frozen.start()
-    own_cot = pltpu.make_async_copy(cot_in_ref.at[:, mine], cot_ref.at[my_rows], own_sems.at[1])
-    own_cot.start()
+    def columns(index, h):
+        return pl.ds(pl.multiple_of(index * c + h * lanes, lanes), lanes)
+
+    def fetch(h):
+        frozens = everyone(
+            9 + slabs + h, lambda peer: frozen_ref.at[:, :, columns(peer, h)], got_frozen.at[h, me]
+        )
+        cots = everyone(
+            9 + 2 * slabs + h,
+            lambda peer: cot_in_ref.at[:, columns(peer, h)],
+            got_cot.at[h, my_rows],
+        )
+        own = keep(5 + h, frozen_ref.at[:, :, columns(me, h)], got_frozen.at[h, me])
+        cots.append(
+            keep(5 + slabs + h, cot_in_ref.at[:, columns(me, h)], got_cot.at[h, my_rows])
+        )
+        return [own] + frozens, cots
+
+    places = everyone(1, lambda peer: pos_ref, place_all.at[me])
+    coming = fetch(0)
     place_all[me] = pos_ref[...]
     low_parts[tp_me] = fdot(down_ref[...], tokens_ref[...], ((1,), (1,)))
     swaps = tp_swap(0, low_parts)
-    cots = everyone(10, lambda peer: cot_in_ref.at[:, part_of(peer, c)], cot_ref.at[my_rows])
+
+    start_col[...] = doc_starts(
+        lax.broadcasted_iota(jnp.int32, start_col.shape, 0), lengths_ref
+    )
+    start_row[...] = doc_starts(
+        lax.broadcasted_iota(jnp.int32, start_row.shape, 1), lengths_ref
+    )
     finish(swaps)
     low_own[...] = tidy(low_parts, low_parts.shape[0]).astype(bf16)
     low_all[me] = low_own[...]
-    lows = everyone(11, lambda peer: low_own, low_all.at[me])
-
-    start_col[...] = doc_starts(
-        lax.broadcasted_iota(jnp.int32, start_col.shape, 0), lengths_ref
-    )
-    start_row[...] = doc_starts(
-        lax.broadcasted_iota(jnp.int32, start_row.shape, 1), lengths_ref
-    )
-
+    lows = everyone(2, lambda peer: low_own, low_all.at[me])
+
+    tap_id = lax.broadcasted_iota(jnp.int32, (taps, wide), 0)
+    spot_id = lax.broadcasted_iota(jnp.int32, (taps, wide), 1)
+    own_filter = filter_ref[part_of(me, groups), :]
+    taps_f[...] = fdot(own_filter, jnp.where(tap_id + spot_id == taps, 1.0, 0.0).astype(bf16))
+    taps_b[...] = fdot(own_filter, jnp.where(tap_id == spot_id, 1.0, 0.0).astype(bf16))
     for g in range(groups):
         span = slice(g * taps, (g + 1) * taps)
-        for taps_ref, bank in ((taps_f_ref, bank_f), (taps_b_ref, bank_b)):
+        for taps_ref, bank in ((taps_f, bank_f), (taps_b, bank_b)):
             line = jnp.broadcast_to(taps_ref[g : g + 1, :], (taps, wide))
             bank[span, :] = pltpu.roll(line, 0, 1, stride=1, stride_axis=0).astype(bf16)
-
+    finish(places)
+
+    @pl.loop(0, shards)
+    def _(w):
+        base = pl.multiple_of(w * rows, rows)
+        spot = lax.broadcasted_iota(jnp.int32, (rows, rows), 0) + base
+        for j in range(shards):
+            hot_ref[pl.ds(base, rows), j * rows : (j + 1) * rows] = jnp.where(
+                place_all[j] == spot, 1.0, 0.0
+            ).astype(bf16)
+
+    pre[:EDGE, :] = jnp.zeros((EDGE, width), bf16)
+    prod[:taps, :] = jnp.zeros((taps, lanes), bf16)
+    back[n:, :] = jnp.zeros((taps, lanes), bf16)
+    back_post[n:, :] = jnp.zeros((EDGE, width), bf16)
+    small_own[...] = jnp.zeros_like(small_own)
     unit = jnp.where(
         lax.broadcasted_iota(jnp.int32, (rank, LANES), 0)
         == lax.broadcasted_iota(jnp.int32, (rank, LANES), 1),
         1.0,
         0.0,
     ).astype(bf16)
-
-    finish(places)
-    finish(lows)
-    for d in range(shards):
-        if d == 0:
-            own_frozen.wait()
-        else:
-            frozens[d - 1].wait()
-        j = lax.rem(me + shards - d, shards)
-        at = part_of(j, rows)
-        low = fdot(low_all[j], unit, ((0,), (0,))).astype(bf16)
-        for a in range(kinds):
-            cols = slice(a * c, (a + 1) * c)
-            rhs[at, cols] = (got_frozen[j, a].astype(f32) + fdot(low, up_ref[:, cols])).astype(bf16)
-        rhs[at, width:] = low
-
-    pre[:EDGE, :] = jnp.zeros((EDGE, width), bf16)
-    tall = rows * 2
-
-    @pl.loop(0, n // tall)
-    def _(w):
-        base = pl.multiple_of(w * tall, tall)
-        spot = lax.broadcasted_iota(jnp.int32, (tall, rows), 0) + base
-        hot = jnp.concatenate(
-            [jnp.where(place_all[j] == spot, 1.0, 0.0).astype(bf16) for j in range(shards)], axis=1
-        )
-        moved = fdot(hot, rhs[...]).astype(bf16)
-        pre[pl.ds(pl.multiple_of(base + EDGE, EDGE), tall), :] = moved[:, :width]
-        low_win[pl.ds(base, tall), :] = moved[:, width:]
-
-    own_cot.wait()
-    finish(cots)
-    prod[:taps, :] = jnp.zeros((taps, c), bf16)
-    back[n:, :] = jnp.zeros((taps, c), bf16)
-
-    @pl.loop(0, blocks)
-    def _(b):
-        base = pl.multiple_of(b * taps, taps)
-        at = pl.ds(base, taps)
-        ext = pre[pl.ds(base, taps + EDGE), :].astype(f32)
-        off = lax.broadcasted_iota(jnp.int32, (taps, 1), 0) + base - start_col[at, :]
-        total = jnp.zeros((taps, width), f32)
-        for s in range(shorts):
-            gate = (off >= s).astype(f32)
-            total = total + short_ref[s : s + 1, :] * ext[EDGE - s : EDGE - s + taps] * gate
-        rounded = total.astype(bf16)
-        post[at, :] = rounded
-        rounded = rounded.astype(f32)
-        prod[pl.ds(pl.multiple_of(base + taps, taps), taps), :] = (
-            rounded[:, c : 2 * c] * rounded[:, 2 * c :]
-        ).astype(bf16)
-        back[at, :] = (cot_ref[at, :].astype(f32) * rounded[:, :c]).astype(bf16)
-
-    pair_acc[...] = jnp.zeros_like(pair_acc)
-    short_grad_ref[...] = jnp.zeros_like(short_grad_ref)
-    back_post[n:, :] = jnp.zeros((EDGE, width), bf16)
-    lane_group = lax.broadcasted_iota(jnp.int32, (taps, c), 1) // per
-
+    lane_group = lax.broadcasted_iota(jnp.int32, (taps, lanes), 1) // per
+    sel = [jnp.where(lane_group == g, 1.0, 0.0).astype(bf16) for g in range(some)]
     turned = wide - 1 - lax.broadcasted_iota(jnp.int32, (taps, wide), 1)
     flip = jnp.where(
         lax.broadcasted_iota(jnp.int32, (wide, wide), 0)
@@ -265,134 +248,191 @@
 
     def pick(stacked):
         chosen = stacked[:taps]
-        for g in range(1, groups):
+        for g in range(1, some):
             chosen = jnp.where(lane_group == g, stacked[g * taps : (g + 1) * taps], chosen)
         return chosen
 
-    @pl.loop(0, blocks)
-    def _(b):
-        base = pl.multiple_of(b * taps, taps)
-        at = pl.ds(base, taps)
-        window = prod[pl.ds(base, 2 * taps), :]
-        ahead = back[pl.ds(base, 2 * taps), :]
-        col_pos = lax.broadcasted_iota(jnp.int32, (taps, wide), 1) + (base - taps)
-        same_f = col_pos >= start_col[at, :]
-        gate_f = jnp.where(same_f, 1.0, 0.0).astype(bf16)
-        gate_r = jnp.where(turned + (base - taps) >= start_col[at, :], 1.0, 0.0)
-        row_pos = lax.broadcasted_iota(jnp.int32, (taps, wide), 0) + base
-        same_b = row_pos >= start_row[:, pl.ds(base, wide)]
-        gate_b = jnp.where(same_b, 1.0, 0.0).astype(bf16)
-        many_f = jnp.concatenate([gate_f] * groups, axis=0)
-        many_b = jnp.concatenate([gate_b] * groups, axis=0)
-        conv = pick(fdot(bank_f[...] * many_f, window))
-        spread = pick(fdot(bank_b[...] * many_b, ahead))
-        here = ahead[:taps]
-        split = jnp.concatenate(
-            [jnp.where(lane_group == g, here, jnp.zeros_like(here)) for g in range(groups)], axis=0
-        )
-        pairs = fdot(split, fdot(flip, window).astype(bf16), ((1,), (1,)))
-        for g in range(groups):
+    finish(lows)
+    outs = []
+    for h in range(slabs):
+        frozens, cots = coming
+        here = columns(me, h)
+        slab = slice(h * lanes, (h + 1) * lanes)
+        bank_rows = slice(h * some * taps, (h + 1) * some * taps)
+        short_rows = [
+            jnp.concatenate([short_ref[s * kinds + a : s * kinds + a + 1, here] for a in range(kinds)], axis=1)
+            for s in range(shorts)
+        ]
+        up_parts = [up_ref[a, :, here] for a in range(kinds)]
+        skip = skip_ref[:, here]
+
+        for d in range(shards):
+            frozens[d].wait()
+            j = lax.rem(me + shards - d, shards)
+            at = part_of(j, rows)
+            low = low_all[j]
+            for a in range(kinds):
+                cols = slice(a * lanes, (a + 1) * lanes)
+                rhs[at, cols] = (
+                    got_frozen[h, j, a].astype(f32) + fdot(low, up_parts[a], ((0,), (0,)))
+                ).astype(bf16)
+            if h == 0:
+                rhs[at, width:] = fdot(low, unit, ((0,), (0,))).astype(bf16)
+        if h + 1 < slabs:
+            coming = fetch(h + 1)
+        tall = rows * 2
+
+        @pl.loop(0, n // tall)
+        def _(w):
+            base = pl.multiple_of(w * tall, tall)
+            at = pl.ds(base, tall)
+            to = pl.ds(pl.multiple_of(base + EDGE, EDGE), tall)
+            if h == 0:
+                moved = fdot(hot_ref[at, :], rhs[...]).astype(bf16)
+                pre[to, :] = moved[:, :width]
+                low_win[at, :] = moved[:, width:]
+            else:
+                pre[to, :] = fdot(hot_ref[at, :], rhs[:, :width]).astype(bf16)
+
+        finish(cots)
+
+        @pl.loop(0, blocks)
+        def _(b):
+            base = pl.multiple_of(b * taps, taps)
+            at = pl.ds(base, taps)
+            ext = pre[pl.ds(base, taps + EDGE), :].astype(f32)
+            off = lax.broadcasted_iota(jnp.int32, (taps, 1), 0) + base - start_col[at, :]
+            total = jnp.zeros((taps, width), f32)
+            for s in range(shorts):
+                gate = (off >= s).astype(f32)
+                total = total + short_rows[s] * ext[EDGE - s : EDGE - s + taps] * gate
+            rounded = total.astype(bf16)
+            post[at, :] = rounded
+            rounded = rounded.astype(f32)
+            prod[pl.ds(pl.multiple_of(base + taps, taps), taps), :] = (
+                rounded[:, lanes : 2 * lanes] * rounded[:, 2 * lanes :]
+            ).astype(bf16)
+            back[at, :] = (got_cot[h, at, :].astype(f32) * rounded[:, :lanes]).astype(bf16)
+
+        pair_acc[...] = jnp.zeros_like(pair_acc)
+
+        @pl.loop(0, blocks)
+        def _(b):
+            base = pl.multiple_of(b * taps, taps)
+            at = pl.ds(base, taps)
+            window = prod[pl.ds(base, 2 * taps), :]
+            ahead = back[pl.ds(base, 2 * taps), :]
+            begin = start_col[at, :]
+            col_pos = lax.broadcasted_iota(jnp.int32, (taps, wide), 1) + (base - taps)
+            gate_f = jnp.where(col_pos >= begin, 1.0, 0.0).astype(bf16)
+            gate_r = jnp.where(turned + (base - taps) >= begin, 1.0, 0.0)
+            row_pos = lax.broadcasted_iota(jnp.int32, (taps, wide), 0) + base
+            gate_b = jnp.where(row_pos >= start_row[:, pl.ds(base, wide)], 1.0, 0.0).astype(bf16)
+            many_f = jnp.concatenate([gate_f] * some, axis=0)
+            many_b = jnp.concatenate([gate_b] * some, axis=0)
+            conv = pick(fdot(bank_f[bank_rows, :] * many_f, window))
+            spread = pick(fdot(bank_b[bank_rows, :] * many_b, ahead))
+            back_here = ahead[:taps]
+            split = jnp.concatenate([back_here * sel[g] for g in range(some)], axis=0)
+            pairs = fdot(split, fdot(flip, window).astype(bf16), ((1,), (1,)))
+            for g in range(some):
+                span = slice(g * taps, (g + 1) * taps)
+                pair_acc[span, :] += pairs[span] * gate_r
+            product = window[taps:].astype(f32)
+            cot = got_cot[h, at, :].astype(f32)
+            query = post[at, :lanes].astype(f32)
+            key = post[at, lanes : 2 * lanes].astype(f32)
+            value = post[at, 2 * lanes :].astype(f32)
+            gated = cot * query
+            direct = conv + skip * product
+            out_buf[h, at, :] = (query * direct).astype(bf16)
+            product_back = spread + skip * gated
+            skip_row = shorts * kinds
+            small_own[skip_row : skip_row + 1, slab] += jnp.sum(gated * product, axis=0, keepdims=True)
+            back_post[at, :lanes] = (cot * direct).astype(bf16)
+            back_post[at, lanes : 2 * lanes] = (product_back * value).astype(bf16)
+            back_post[at, 2 * lanes :] = (product_back * key).astype(bf16)
+
+        outs += everyone(
+            9 + h, lambda peer: out_buf.at[h, part_of(peer, rows)], mixer_out.at[:, here]
+        )
+        outs.append(keep(5 + 2 * slabs + h, out_buf.at[h, my_rows], mixer_out.at[:, here]))
+
+        for g in range(some):
             span = slice(g * taps, (g + 1) * taps)
-            pair_acc[span, :] += pairs[span] * gate_r
-        product = window[taps:].astype(f32)
-        cot = cot_ref[at, :].astype(f32)
-        query = post[at, :c].astype(f32)
-        key = post[at, c : 2 * c].astype(f32)
-        value = post[at, 2 * c :].astype(f32)
-        gated = cot * query
-        skip = skip_ref[...]
-        direct = conv + skip * product
-        out_ref[at, :] = (query * direct).astype(bf16)
-        product_back = spread + skip * gated
-        short_grad_ref[shorts : shorts + 1, :c] += jnp.sum(gated * product, axis=0, keepdims=True)
-        back_post[at, :c] = (cot * direct).astype(bf16)
-        back_post[at, c : 2 * c] = (product_back * value).astype(bf16)
-        back_post[at, 2 * c :] = (product_back * key).astype(bf16)
-
-    copies = everyone(1, lambda peer: out_ref.at[part_of(peer, rows)], mixer_out.at[:, mine])
-    own = [pltpu.make_async_copy(out_ref.at[my_rows], mixer_out.at[:, mine], own_sems.at[0])]
-    own[0].start()
-    for g in range(groups):
-        span = slice(g * taps, (g + 1) * taps)
-        square = pltpu.roll(pair_acc[span, :], wide - taps + 1, 1, stride=1, stride_axis=0)
-        long_grad_ref[g : g + 1, :] = jnp.sum(square[:, :taps], axis=0, keepdims=True)
-
-    @pl.loop(0, blocks)
-    def _(b):
-        base = pl.multiple_of(b * taps, taps)
-        at = pl.ds(base, taps)
-        ext = pre[pl.ds(base, taps + EDGE), :].astype(f32)
-        back_ext = back_post[pl.ds(base, taps + EDGE), :].astype(f32)
-        off = (
-            lax.broadcasted_iota(jnp.int32, (taps + EDGE, 1), 0)
-            + base
-            - start_col[pl.ds(base, taps + EDGE), :]
-        )
-        total = jnp.zeros((taps, width), f32)
-        for s in range(shorts):
-            masked = back_ext * (off >= s).astype(f32)
-            total = total + short_ref[s : s + 1, :] * masked[s : s + taps]
-            short_grad_ref[s : s + 1, :] += jnp.sum(
-                masked[:taps] * ext[EDGE - s : EDGE - s + taps], axis=0, keepdims=True
+            square = pltpu.roll(pair_acc[span, :], wide - taps + 1, 1, stride=1, stride_axis=0)
+            row = h * some + g
+            long_own[row : row + 1, :] = jnp.sum(square[:, :taps], axis=0, keepdims=True)
+
+        @pl.loop(0, blocks)
+        def _(b):
+            base = pl.multiple_of(b * taps, taps)
+            at = pl.ds(base, taps)
+            ext = pre[pl.ds(base, taps + EDGE), :].astype(f32)
+            back_ext = back_post[pl.ds(base, taps + EDGE), :].astype(f32)
+            off = (
+                lax.broadcasted_iota(jnp.int32, (taps + EDGE, 1), 0)
+                + base
+                - start_col[pl.ds(base, taps + EDGE), :]
             )
-        rhs[at, :width] = total.astype(bf16)
-
-    back_pre = rhs[:, :width]
-    up_grad = fdot(low_win[...], back_pre, ((0,), (0,)))
-    for a in range(kinds):
-        up_grad_ref[a] = up_grad[:rank, a * c : (a + 1) * c]
-    back_low_ref[...] = fdot(up_ref[:rank, :], back_pre, ((1,), (1,)))
-    reduce_low = everyone(0, lambda peer: back_low_ref.at[:, part_of(peer, rows)], low_got.at[me])
-    low_got[me] = back_low_ref[:, my_rows]
-    copies += everyone(2, lambda peer: up_grad_ref, grad_up.at[:, :, mine])
-    copies += everyone(3, lambda peer: short_grad_ref, grad_small.at[me])
-    copies += everyone(4, lambda peer: long_grad_ref, grad_long.at[part_of(me, groups)])
-    own += [
-        pltpu.make_async_copy(up_grad_ref, grad_up.at[:, :, mine], own_sems.at[1]),
-        pltpu.make_async_copy(short_grad_ref, grad_small.at[me], own_sems.at[2]),
-        pltpu.make_async_copy(long_grad_ref, grad_long.at[part_of(me, groups)], own_sems.at[3]),
-    ]
-    for copy in own[1:]:
-        copy.start()
+            total = jnp.zeros((taps, width), f32)
+            for s in range(shorts):
+                masked = back_ext * (off >= s).astype(f32)
+                total = total + short_rows[s] * masked[s : s + taps]
+                sums = jnp.sum(
+                    masked[:taps] * ext[EDGE - s : EDGE - s + taps], axis=0, keepdims=True
+                )
+                for a in range(kinds):
+                    row = s * kinds + a
+                    small_own[row : row + 1, slab] += sums[:, a * lanes : (a + 1) * lanes]
+            rhs[at, :width] = total.astype(bf16)
+
+        back_pre = rhs[:, :width]
+        low_term = fdot(jnp.concatenate(up_parts, axis=1), back_pre, ((1,), (1,)))
+        back_low[...] = low_term if h == 0 else back_low[...] + low_term
+        if h + 1 == slabs:
+            reduce_low = everyone(0, lambda peer: back_low.at[:, part_of(peer, rows)], low_got.at[me])
+            low_got[me] = back_low[:, my_rows]
+        up_term = fdot(low_win[...], back_pre, ((0,), (0,)))
+        for a in range(kinds):
+            up_own[a, :, slab] = up_term[:rank, a * lanes : (a + 1) * lanes]
+
+    copies = everyone(3, lambda peer: up_own, grad_up.at[:, :, mine])
+    copies += everyone(4, lambda peer: small_own, grad_small.at[:, mine])
+    copies += everyone(5, lambda peer: long_own, grad_long.at[part_of(me, groups)])
+    copies += outs
+    copies.append(keep(1, up_own, grad_up.at[:, :, mine]))
+    copies.append(keep(2, small_own, grad_small.at[:, mine]))
+    copies.append(keep(3, long_own, grad_long.at[part_of(me, groups)]))
     finish(reduce_low)
-    total = low_got[0]
-    for j in range(1, shards):
-        total = total + low_got[j]
-    back_parts[tp_me] = total
+    back_parts[tp_me] = tidy(low_got, shards)
     finish(tp_swap(1, back_parts))
-    total = back_parts[0]
-    for t in range(1, back_parts.shape[0]):
-        total = total + back_parts[t]
-    back_own_low[...] = total.astype(bf16)
-    spread = everyone(5, lambda peer: back_own_low, back_all.at[me])
-    back_all[me] = total.astype(bf16)
-    finish(spread)
-    back_own = jnp.zeros((rank, rows), jnp.float32)
+    back_own_low[...] = tidy(back_parts, back_parts.shape[0]).astype(bf16)
+    back_all[me] = back_own_low[...]
+    finish(everyone(6, lambda peer: back_own_low, back_all.at[me]))
+    back_own = jnp.zeros((rank, rows), f32)
     for j in range(shards):
         spot = lax.broadcasted_iota(jnp.int32, (rows, rows), 0) + j * rows
         hot = jnp.where(pos_ref[...] == spot, 1.0, 0.0).astype(bf16)
         back_own = back_own + fdot(back_all[j], hot)
     down_part[...] = fdot(back_own.astype(bf16), tokens_ref[...])
-    reduce_down = everyone(6, lambda peer: down_part.at[:, part_of(peer, c)], down_got.at[me])
+    reduce_down = everyone(7, lambda peer: down_part.at[:, part_of(peer, c)], down_got.at[me])
     down_got[me] = down_part[:, mine]
     finish(reduce_down)
-    total = down_got[0]
-    for j in range(1, shards):
-        total = total + down_got[j]
-    down_own[...] = total
-    copies += everyone(7, lambda peer: down_own, grad_down.at[:, mine])
-    last = pltpu.make_async_copy(down_own, grad_down.at[:, mine], own_sems.at[4])
-    last.start()
-    finish(copies + own + [last])
-
-
-def mixer(lengths, frozen, cot, tokens, down, pos, up, short, taps_f, taps_b, skip):
+    down_own[...] = tidy(down_got, shards)
+    copies += everyone(8, lambda peer: down_own, grad_down.at[:, mine])
+    copies.append(keep(4, down_own, grad_down.at[:, mine]))
+    finish(copies)
+
+
+def mixer(lengths, frozen, cot, tokens, down, pos, up, short, long_filter, skip):
     kinds, rows, channels = frozen.shape
     shards, tps = lax.axis_size("ctx"), lax.axis_size("tp")
     n, c = rows * shards, channels // shards
-    groups, wide = taps_f.shape
-    taps = wide // 2
-    width = kinds * c
+    slabs, lanes = c // LANES, LANES
+    taps = long_filter.shape[1]
+    groups, wide = long_filter.shape[0] // shards, 2 * taps
+    width = kinds * lanes
     rank = down.shape[0]
     small = -(-(short.shape[0] + 1) // 8) * 8
     f32, bf16, i32 = jnp.float32, jnp.bfloat16, jnp.int32
@@ -404,19 +444,19 @@
             shape((rows, channels), bf16),
             shape((rank, channels), f32),
             shape((kinds, rank, channels), f32),
-            shape((shards, small, width), f32),
+            shape((small, channels), f32),
             shape((shards * groups, taps), f32),
         ),
-        in_specs=[pl.BlockSpec(memory_space=pltpu.SMEM), hbm, hbm] + [vmem] * 8,
+        in_specs=[pl.BlockSpec(memory_space=pltpu.SMEM), hbm, hbm] + [vmem] * 7,
         out_specs=(hbm,) * 5,
         scratch_shapes=[
-            pltpu.VMEM((shards, kinds, rows, c), bf16),
-            pltpu.VMEM((n, c), bf16),
+            pltpu.VMEM((slabs, shards, kinds, rows, lanes), bf16),
+            pltpu.VMEM((slabs, n, lanes), bf16),
             pltpu.VMEM((shards, rank, rows), bf16),
             pltpu.VMEM((shards, 1, rows), i32),
-            pltpu.VMEM((n, c), bf16),
+            pltpu.VMEM((slabs, n, lanes), bf16),
             pltpu.VMEM((kinds, rank, c), f32),
-            pltpu.VMEM((small, width), f32),
+            pltpu.VMEM((small, c), f32),
             pltpu.VMEM((groups, taps), f32),
             pltpu.VMEM((rank, n), f32),
             pltpu.VMEM((shards, rank, rows), f32),
@@ -428,21 +468,24 @@
             pltpu.VMEM((rank, c), f32),
             pltpu.VMEM((tps, rank, rows), f32),
             pltpu.VMEM((rank, rows), bf16),
+            pltpu.VMEM((n, n), bf16),
             pltpu.VMEM((n, width + LANES), bf16),
             pltpu.VMEM((n + EDGE, width), bf16),
             pltpu.VMEM((n, LANES), bf16),
             pltpu.VMEM((n, width), bf16),
-            pltpu.VMEM((n + taps, c), bf16),
-            pltpu.VMEM((n + taps, c), bf16),
+            pltpu.VMEM((n + taps, lanes), bf16),
+            pltpu.VMEM((n + taps, lanes), bf16),
             pltpu.VMEM((n + EDGE, width), bf16),
+            pltpu.VMEM((groups, wide), f32),
+            pltpu.VMEM((groups, wide), f32),
             pltpu.VMEM((groups * taps, wide), bf16),
             pltpu.VMEM((groups * taps, wide), bf16),
-            pltpu.VMEM((groups * taps, wide), f32),
+            pltpu.VMEM((groups // slabs * taps, wide), f32),
             pltpu.VMEM((n + EDGE, 1), i32),
             pltpu.VMEM((1, n + taps), i32),
-            pltpu.SemaphoreType.DMA((12, shards)),
-            pltpu.SemaphoreType.DMA((12, shards)),
-            pltpu.SemaphoreType.DMA((5,)),
+            pltpu.SemaphoreType.DMA((9 + 3 * slabs, shards)),
+            pltpu.SemaphoreType.DMA((9 + 3 * slabs, shards)),
+            pltpu.SemaphoreType.DMA((5 + 3 * slabs,)),
             pltpu.SemaphoreType.DMA((2, tps)),
             pltpu.SemaphoreType.DMA((2, tps)),
         ],
@@ -452,7 +495,7 @@
         cost_estimate=pl.CostEstimate(
             flops=8 * n * groups * taps * wide, bytes_accessed=16 * n * c, transcendentals=0
         ),
-    )(lengths, frozen, cot, tokens, down, pos, up, short, taps_f, taps_b, skip)
+    )(lengths, frozen, cot, tokens, down, pos, up, short, long_filter, skip)
 
 
 def by_channels(
@@ -467,48 +510,28 @@
     document_lengths,
     window_row_position,
 ):
-    f32, bf16 = jnp.float32, jnp.bfloat16
-    rows, channels = tokens.shape
-    kinds = frozen.shape[1]
-    rank = adapter_down_weight.shape[0]
-    shorts = short_depthwise_filter.shape[0]
-    shards = lax.axis_size("ctx")
-    me = lax.axis_index("ctx")
-    n = rows * shards
-    c = channels // shards
-    taps = long_group_filter.shape[1]
-    groups = long_group_filter.shape[0] // shards
-    pos = window_row_position[None, :]
-    def own(array):
-        return lax.dynamic_slice_in_dim(array, me * c, c, array.ndim - 1)
-
-    up = jnp.pad(own(adapter_up_weight).reshape(rank, kinds * c), ((0, LANES - rank), (0, 0)))
-    short = own(short_depthwise_filter).reshape(shorts, kinds * c).astype(f32)
-    skip = own(skip_direct_scale)[None, :]
-    bank = lax.dynamic_slice_in_dim(long_group_filter, me * groups, groups, 0).astype(f32)
-    taps_f = jnp.pad(bank[:, ::-1], ((0, 0), (1, taps - 1)))
-    taps_b = jnp.pad(bank, ((0, 0), (0, taps)))
+    channels = tokens.shape[1]
+    shorts, kinds, _ = short_depthwise_filter.shape
+    count = shorts * kinds
     mixer_out, grad_down, grad_up, grad_small, grad_long = mixer(
         document_lengths,
         frozen.transpose(1, 0, 2),
         cotangent,
         tokens,
         adapter_down_weight,
-        pos,
-        up,
-        short,
-        taps_f,
-        taps_b,
-        skip,
-    )
-    grad_short = grad_small[:, :shorts].reshape(shards, shorts, kinds, c).transpose(1, 2, 0, 3)
+        window_row_position[None, :],
+        adapter_up_weight.transpose(1, 0, 2),
+        short_depthwise_filter.reshape(count, channels).astype(jnp.float32),
+        long_group_filter,
+        skip_direct_scale[None, :],
+    )
     return (
         mixer_out,
         grad_down,
         grad_up.transpose(1, 0, 2),
-        grad_short.reshape(shorts, kinds, channels),
+        grad_small[:count].reshape(shorts, kinds, channels),
         grad_long,
-        grad_small[:, shorts, :c].reshape(channels),
+        grad_small[count],
     )
 
 

time: 149 us -> 129 us (0.87)
  Pallas kernels: 133 us -> 117 us
  local copies, waits for them, and re-layouts: 13.3 us -> 10.8 us
    pallas_call x1, Pallas kernels: 133 us -> 117 us  [mixer(): pl.pallas_call(mixer_kernel, out_shape=(shape((rows, channels), bf16), sh...]
    pad x3 -> x0, local copies, waits for them, and re-layouts: 1.98 us -> none  [the longest x1 0.69 us: by_channels(): jnp.pad(own(adapter_up_weight).reshape(rank, kinds * c), ((0, LANES - ran...]
    unnamed x12 -> x6, local copies, waits for them, and re-layouts: 6.78 us -> 6.27 us
where the time goes in v2:
time: 129 us
  Pallas kernels  117 us (91%)
  local copies, waits for them, and re-layouts  10.8 us (8%)
    pallas_call x1, Pallas kernels, mixer(): pl.pallas_call(mixer_kernel, out_shape=(shape((rows, channels), bf16), sh...  117 us
    unnamed x6, local copies, waits for them, and re-layouts  6.27 us

profile of v2, /device:TPU:0, one launch (start us, length us, event | category | flops | bytes accessed | tf_op | source)
XLA Modules:
  0.0 128.7 jit_solution(751407398088179841)
XLA Ops:
  0.6 1.5 %reshape.19.short_ref = f32[9,2048]{1,0:T(8,128)} reshape(bf16[3,3,2048]{2,1,0:T(4,128)(2,1)} %param.15) | data formatting | bytes 110592 | tf_op jit(solution)/shard_map/convert_element_type | solution.py:524
  2.1 117.3 %shard_map.145 = (bf16[256,2048]{1,0:T(8,128)(2,1)}, f32[16,2048]{1,0:T(8,128)}, f32[3,16,2048]{2,1,0:T(8,128)}, f32[16,2048]{1,0:T(8,128)}, f32[128,128]{1,0:T(8,128)}) custom-call(s32[16]{0:T(128)} %lengths_ref.1, bf16[3,256,2048]{2,1,0:T(8,128)(2,1)} %bitcast.10, bf16[256,2048]{1,0:T(8,128)(2,1)} %cot_in_ref.1, bf16[256,2048]{1,0:T(8,128)(2,1)} %tokens_ref.1, ...), custom_call_target="tpu_custom_call" | custom-call | flops 8589934592 | bytes 8388608 | tf_op jit(solution)/shard_map/pallas_call | solution.py:441
  119.4 0.0 copy-start
  119.4 1.6 %reshape.18 = f32[3,3,2048]{2,1,0:T(4,128)} reshape(f32[9,2048]{1,0:T(8,128)} %bitcast.8) | data formatting | bytes 147456 | tf_op jit(solution)/shard_map/reshape | solution.py:532
  121.0 1.4 %slice.7 = f32[1,2048]{1,0:T(1,128)} slice(f32[16,2048]{1,0:T(8,128)} %get-tuple-element.14), slice={[9:10], [0:2048]} | slice | bytes 16384 | tf_op jit(solution)/shard_map/slice | solution.py:534
  122.5 2.3 %copy.20 = bf16[256,2048]{1,0:T(8,128)(2,1)} copy(bf16[256,2048]{1,0:T(8,128)(2,1)} %get-tuple-element.22) | data formatting | bytes 2097152
  124.8 1.6 %copy.21 = f32[16,2048]{1,0:T(8,128)} copy(f32[16,2048]{1,0:T(8,128)} %get-tuple-element.23) | data formatting | bytes 262144
  126.3 1.8 %copy.22 = f32[16,3,2048]{2,0,1:T(8,128)} copy(f32[16,3,2048]{2,0,1:T(8,128)} %bitcast.7) | data formatting | bytes 786432
  128.1 0.0 copy-done
  128.1 0.6 copy.23
Async XLA Ops:
  119.4 8.7 %copy-start = (f32[128,128]{1,0:T(8,128)S(1)}, f32[128,128]{1,0:T(8,128)}, u32[]{:S(2)}) copy-start(f32[128,128]{1,0:T(8,128)} %get-tuple-element.26) | copy-start | bytes 196612

commit v3 on v2

--- a/solution.py
+++ b/solution.py
@@ -126,7 +126,7 @@
     some = groups // slabs
     width = kinds * lanes
     blocks = n // taps
-    shorts = short_ref.shape[0] // kinds
+    shorts = short_ref.shape[0]
     rank = down_ref.shape[0]
     f32, bf16 = jnp.float32, jnp.bfloat16
     me, peers = ctx_peers()
@@ -171,23 +171,22 @@
     def columns(index, h):
         return pl.ds(pl.multiple_of(index * c + h * lanes, lanes), lanes)
 
-    def fetch(h):
-        frozens = everyone(
+    def fetch_frozen(h):
+        own = keep(5 + h, frozen_ref.at[:, :, columns(me, h)], got_frozen.at[h, me])
+        return [own] + everyone(
             9 + slabs + h, lambda peer: frozen_ref.at[:, :, columns(peer, h)], got_frozen.at[h, me]
         )
-        cots = everyone(
+
+    def fetch_cot(h):
+        own = keep(5 + slabs + h, cot_in_ref.at[:, columns(me, h)], got_cot.at[h, my_rows])
+        return [own] + everyone(
             9 + 2 * slabs + h,
             lambda peer: cot_in_ref.at[:, columns(peer, h)],
             got_cot.at[h, my_rows],
         )
-        own = keep(5 + h, frozen_ref.at[:, :, columns(me, h)], got_frozen.at[h, me])
-        cots.append(
-            keep(5 + slabs + h, cot_in_ref.at[:, columns(me, h)], got_cot.at[h, my_rows])
-        )
-        return [own] + frozens, cots
 
     places = everyone(1, lambda peer: pos_ref, place_all.at[me])
-    coming = fetch(0)
+    coming = fetch_frozen(0)
     place_all[me] = pos_ref[...]
     low_parts[tp_me] = fdot(down_ref[...], tokens_ref[...], ((1,), (1,)))
     swaps = tp_swap(0, low_parts)
@@ -255,14 +254,16 @@
     finish(lows)
     outs = []
     for h in range(slabs):
-        frozens, cots = coming
+        frozens = coming
         here = columns(me, h)
         slab = slice(h * lanes, (h + 1) * lanes)
         bank_rows = slice(h * some * taps, (h + 1) * some * taps)
-        short_rows = [
-            jnp.concatenate([short_ref[s * kinds + a : s * kinds + a + 1, here] for a in range(kinds)], axis=1)
-            for s in range(shorts)
-        ]
+        short_rows = []
+        for s in range(shorts):
+            lines = short_ref[s, :, here].astype(f32)
+            short_rows.append(
+                jnp.concatenate([lines[a : a + 1] for a in range(kinds)], axis=1)
+            )
         up_parts = [up_ref[a, :, here] for a in range(kinds)]
         skip = skip_ref[:, here]
 
@@ -278,8 +279,8 @@
                 ).astype(bf16)
             if h == 0:
                 rhs[at, width:] = fdot(low, unit, ((0,), (0,))).astype(bf16)
-        if h + 1 < slabs:
-            coming = fetch(h + 1)
+        if h == 0:
+            cots = fetch_cot(0)
         tall = rows * 2
 
         @pl.loop(0, n // tall)
@@ -295,6 +296,9 @@
                 pre[to, :] = fdot(hot_ref[at, :], rhs[:, :width]).astype(bf16)
 
         finish(cots)
+        if h + 1 < slabs:
+            coming = fetch_frozen(h + 1)
+            cots = fetch_cot(h + 1)
 
         @pl.loop(0, blocks)
         def _(b):
@@ -358,12 +362,6 @@
         )
         outs.append(keep(5 + 2 * slabs + h, out_buf.at[h, my_rows], mixer_out.at[:, here]))
 
-        for g in range(some):
-            span = slice(g * taps, (g + 1) * taps)
-            square = pltpu.roll(pair_acc[span, :], wide - taps + 1, 1, stride=1, stride_axis=0)
-            row = h * some + g
-            long_own[row : row + 1, :] = jnp.sum(square[:, :taps], axis=0, keepdims=True)
-
         @pl.loop(0, blocks)
         def _(b):
             base = pl.multiple_of(b * taps, taps)
@@ -396,6 +394,12 @@
         up_term = fdot(low_win[...], back_pre, ((0,), (0,)))
         for a in range(kinds):
             up_own[a, :, slab] = up_term[:rank, a * lanes : (a + 1) * lanes]
+
+        for g in range(some):
+            span = slice(g * taps, (g + 1) * taps)
+            square = pltpu.roll(pair_acc[span, :], wide - taps + 1, 1, stride=1, stride_axis=0)
+            row = h * some + g
+            long_own[row : row + 1, :] = jnp.sum(square[:, :taps], axis=0, keepdims=True)
 
     copies = everyone(3, lambda peer: up_own, grad_up.at[:, :, mine])
     copies += everyone(4, lambda peer: small_own, grad_small.at[:, mine])
@@ -434,7 +438,7 @@
     groups, wide = long_filter.shape[0] // shards, 2 * taps
     width = kinds * lanes
     rank = down.shape[0]
-    small = -(-(short.shape[0] + 1) // 8) * 8
+    small = -(-(short.shape[0] * kinds + 1) // 8) * 8
     f32, bf16, i32 = jnp.float32, jnp.bfloat16, jnp.int32
     shape = jax.ShapeDtypeStruct
     vmem, hbm = pl.BlockSpec(memory_space=pltpu.VMEM), pl.BlockSpec(memory_space=pl.ANY)
@@ -498,6 +502,46 @@
     )(lengths, frozen, cot, tokens, down, pos, up, short, long_filter, skip)
 
 
+def settle_kernel(
+    mixer_in, down_in, up_in, small_ref, long_in, mixer_out, down_out, up_out, short_ref, skip_ref, long_out, sems
+):
+    copies = [
+        pltpu.make_async_copy(mixer_in, mixer_out, sems.at[0]),
+        pltpu.make_async_copy(down_in, down_out, sems.at[1]),
+        pltpu.make_async_copy(up_in, up_out, sems.at[2]),
+        pltpu.make_async_copy(long_in, long_out, sems.at[3]),
+    ]
+    for copy in copies:
+        copy.start()
+    shorts, kinds, _ = short_ref.shape
+    for s in range(shorts):
+        short_ref[s] = small_ref[s * kinds : (s + 1) * kinds, :]
+    skip_ref[...] = small_ref[shorts * kinds : shorts * kinds + 1, :]
+    for copy in copies:
+        copy.wait()
+
+
+def settle(mixer_out, down, up, small, long, shorts, kinds):
+    vmem, hbm = pl.BlockSpec(memory_space=pltpu.VMEM), pl.BlockSpec(memory_space=pl.ANY)
+    channels = mixer_out.shape[1]
+    shape = jax.ShapeDtypeStruct
+    same = [shape(array.shape, array.dtype) for array in (mixer_out, down, up, long)]
+    return pl.pallas_call(
+        settle_kernel,
+        out_shape=(
+            same[0],
+            same[1],
+            same[2],
+            shape((shorts, kinds, channels), jnp.float32),
+            shape((1, channels), jnp.float32),
+            same[3],
+        ),
+        in_specs=[hbm, hbm, hbm, vmem, hbm],
+        out_specs=(hbm, hbm, hbm, vmem, vmem, hbm),
+        scratch_shapes=[pltpu.SemaphoreType.DMA((4,))],
+    )(mixer_out, down, up, small, long)
+
+
 def by_channels(
     tokens,
     frozen,
@@ -510,9 +554,7 @@
     document_lengths,
     window_row_position,
 ):
-    channels = tokens.shape[1]
     shorts, kinds, _ = short_depthwise_filter.shape
-    count = shorts * kinds
     mixer_out, grad_down, grad_up, grad_small, grad_long = mixer(
         document_lengths,
         frozen.transpose(1, 0, 2),
@@ -521,17 +563,20 @@
         adapter_down_weight,
         window_row_position[None, :],
         adapter_up_weight.transpose(1, 0, 2),
-        short_depthwise_filter.reshape(count, channels).astype(jnp.float32),
+        short_depthwise_filter,
         long_group_filter,
         skip_direct_scale[None, :],
+    )
+    mixer_out, grad_down, grad_up, grad_short, grad_skip, grad_long = settle(
+        mixer_out, grad_down, grad_up, grad_small, grad_long, shorts, kinds
     )
     return (
         mixer_out,
         grad_down,
         grad_up.transpose(1, 0, 2),
-        grad_small[:count].reshape(shorts, kinds, channels),
+        grad_short,
         grad_long,
-        grad_small[count],
+        grad_skip[0],
     )
 
 

time: 129 us -> 167 us (1.29)
  Pallas kernels: 117 us -> 166 us
  local copies, waits for them, and re-layouts: 10.8 us -> 0 us
    pallas_call x0 -> x1, Pallas kernels: none -> 52.3 us  [settle(): pl.pallas_call(settle_kernel, out_shape=(same[0], same[1], same[2], shape...]
    unnamed x6 -> x0, local copies, waits for them, and re-layouts: 6.27 us -> none
    pallas_call x1, Pallas kernels: 117 us -> 114 us  [mixer(): pl.pallas_call(mixer_kernel, out_shape=(shape((rows, channels), bf16), sh...]
where the time goes in v3:
time: 167 us
  Pallas kernels  166 us (99%)
    pallas_call x1, Pallas kernels, mixer(): pl.pallas_call(mixer_kernel, out_shape=(shape((rows, channels), bf16), sh...  114 us
    pallas_call x1, Pallas kernels, settle(): pl.pallas_call(settle_kernel, out_shape=(same[0], same[1], same[2], shape...  52.3 us

profile of v3, /device:TPU:0, one launch (start us, length us, event | category | flops | bytes accessed | tf_op | source)
XLA Modules:
  0.0 167.2 jit_solution(18092417378471595648)
XLA Ops:
  0.6 114.1 %shard_map.145 = (bf16[256,2048]{1,0:T(8,128)(2,1)}, f32[16,2048]{1,0:T(8,128)}, f32[3,16,2048]{2,1,0:T(8,128)}, f32[16,2048]{1,0:T(8,128)}, f32[128,128]{1,0:T(8,128)}) custom-call(s32[16]{0:T(128)} %lengths_ref.1, bf16[3,256,2048]{2,1,0:T(8,128)(2,1)} %bitcast.6, bf16[256,2048]{1,0:T(8,128)(2,1)} %cot_in_ref.1, bf16[256,2048]{1,0:T(8,128)(2,1)} %tokens_ref.1, ...), custom_call_target="tpu_custom_call" | custom-call | flops 8589934592 | bytes 8388608 | tf_op jit(solution)/shard_map/pallas_call | solution.py:445
  114.7 52.3 %shard_map.146 = (bf16[256,2048]{1,0:T(8,128)(2,1)}, f32[16,2048]{1,0:T(8,128)}, f32[3,16,2048]{2,1,0:T(8,128)}, f32[3,3,2048]{2,1,0:T(4,128)}, f32[1,2048]{1,0:T(1,128)}, /*index=5*/f32[128,128]{1,0:T(8,128)}) custom-call(bf16[256,2048]{1,0:T(8,128)(2,1)} %get-tuple-element.17.mixer_in, f32[16,2048]{1,0:T(8,128)} %get-tuple-element.18.down_in, ...), custom_call_target="tpu_custom_call" | custom-call | tf_op jit(solution)/shard_map/pallas_call | solution.py:529

commit v4 on v3

--- a/solution.py
+++ b/solution.py
@@ -503,26 +503,23 @@
 
 
 def settle_kernel(
-    mixer_in, down_in, up_in, small_ref, long_in, mixer_out, down_out, up_out, short_ref, skip_ref, long_out, sems
+    mixer_in, down_in, up_in, small_ref, long_in, mixer_out, down_out, up_out, short_ref, skip_ref, long_out
 ):
-    copies = [
-        pltpu.make_async_copy(mixer_in, mixer_out, sems.at[0]),
-        pltpu.make_async_copy(down_in, down_out, sems.at[1]),
-        pltpu.make_async_copy(up_in, up_out, sems.at[2]),
-        pltpu.make_async_copy(long_in, long_out, sems.at[3]),
-    ]
-    for copy in copies:
-        copy.start()
+    for source, target in (
+        (mixer_in, mixer_out),
+        (down_in, down_out),
+        (up_in, up_out),
+        (long_in, long_out),
+    ):
+        target[...] = source[...]
     shorts, kinds, _ = short_ref.shape
     for s in range(shorts):
         short_ref[s] = small_ref[s * kinds : (s + 1) * kinds, :]
     skip_ref[...] = small_ref[shorts * kinds : shorts * kinds + 1, :]
-    for copy in copies:
-        copy.wait()
 
 
 def settle(mixer_out, down, up, small, long, shorts, kinds):
-    vmem, hbm = pl.BlockSpec(memory_space=pltpu.VMEM), pl.BlockSpec(memory_space=pl.ANY)
+    vmem = pl.BlockSpec(memory_space=pltpu.VMEM)
     channels = mixer_out.shape[1]
     shape = jax.ShapeDtypeStruct
     same = [shape(array.shape, array.dtype) for array in (mixer_out, down, up, long)]
@@ -536,9 +533,9 @@
             shape((1, channels), jnp.float32),
             same[3],
         ),
-        in_specs=[hbm, hbm, hbm, vmem, hbm],
-        out_specs=(hbm, hbm, hbm, vmem, vmem, hbm),
-        scratch_shapes=[pltpu.SemaphoreType.DMA((4,))],
+        in_specs=[vmem] * 5,
+        out_specs=(vmem,) * 6,
+        compiler_params=pltpu.CompilerParams(vmem_limit_bytes=16 * 1024 * 1024),
     )(mixer_out, down, up, small, long)
 
 

time: 167 us -> 121 us (0.72)
  Pallas kernels: 166 us -> 115 us
  local copies, waits for them, and re-layouts: 0 us -> 4.86 us
    pallas_call x1, Pallas kernels: 52.3 us -> 1.31 us  [settle(): pl.pallas_call(settle_kernel, out_shape=(same[0], same[1], same[2], shape...]
    unnamed x0 -> x10, local copies, waits for them, and re-layouts: none -> 4.86 us
where the time goes in v4:
time: 121 us
  Pallas kernels  115 us (95%)
  local copies, waits for them, and re-layouts  4.86 us (4%)
    pallas_call x1, Pallas kernels, mixer(): pl.pallas_call(mixer_kernel, out_shape=(shape((rows, channels), bf16), sh...  114 us
    unnamed x10, local copies, waits for them, and re-layouts  4.86 us

profile of v4, /device:TPU:0, one launch (start us, length us, event | category | flops | bytes accessed | tf_op | source)
XLA Modules:
  0.0 120.9 jit_solution(1817279501298356167)
XLA Ops:
  0.6 114.1 %shard_map.145 = (bf16[256,2048]{1,0:T(8,128)(2,1)}, f32[16,2048]{1,0:T(8,128)}, f32[3,16,2048]{2,1,0:T(8,128)}, f32[16,2048]{1,0:T(8,128)}, f32[128,128]{1,0:T(8,128)}) custom-call(s32[16]{0:T(128)} %lengths_ref.1, bf16[3,256,2048]{2,1,0:T(8,128)(2,1)} %bitcast.6, bf16[256,2048]{1,0:T(8,128)(2,1)} %cot_in_ref.1, bf16[256,2048]{1,0:T(8,128)(2,1)} %tokens_ref.1, ...), custom_call_target="tpu_custom_call" | custom-call | flops 8589934592 | bytes 8388608 | tf_op jit(solution)/shard_map/pallas_call | solution.py:445
  114.7 0.0 copy-start
  114.8 1.2 %copy-done = bf16[256,2048]{1,0:T(8,128)(2,1)S(1)} copy-done((bf16[256,2048]{1,0:T(8,128)(2,1)S(1)}, bf16[256,2048]{1,0:T(8,128)(2,1)}, u32[]{:S(2)}) %copy-start) | copy-done | bytes 1048600
  116.0 0.0 copy-start.1
  116.0 1.0 copy-done.1
  117.0 0.0 copy-start.2
  117.0 0.9 copy-done.2
  117.9 0.0 copy-start.3
  117.9 0.9 copy-done.3
  118.8 0.0 copy-start.4
  118.8 0.8 copy-done.4
  119.6 1.3 %shard_map.146 = (bf16[256,2048]{1,0:T(8,128)(2,1)}, f32[16,2048]{1,0:T(8,128)}, f32[3,16,2048]{2,1,0:T(8,128)}, f32[3,3,2048]{2,1,0:T(4,128)}, f32[1,2048]{1,0:T(1,128)}, /*index=5*/f32[128,128]{1,0:T(8,128)}) custom-call(bf16[256,2048]{1,0:T(8,128)(2,1)S(1)} %copy-done, f32[16,2048]{1,0:T(8,128)S(1)} %copy-done.2, f32[3,16,2048]{2,1,0:T(8,128)S(1)} %copy-done.1, ...), custom_call_target="tpu_custom_call" | custom-call | tf_op jit(solution)/shard_map/pallas_call | solution.py:526
Async XLA Ops:
  114.7 1.2 %copy-start = (bf16[256,2048]{1,0:T(8,128)(2,1)S(1)}, bf16[256,2048]{1,0:T(8,128)(2,1)}, u32[]{:S(2)}) copy-start(bf16[256,2048]{1,0:T(8,128)(2,1)} %get-tuple-element.17.mixer_in) | copy-start | bytes 3145732
  116.0 1.0 copy-start.1
  117.0 0.9 copy-start.2
  117.9 0.9 copy-start.3
  118.8 0.8 copy-start.4
